TPU v7x, 32 devices: a whole 2x2x4 slice. The times are simulated.
32 devices in a mesh: dp: 8 (over z, x), segment: 2 (over core), mp: 2 (over y).
Axes of the slice: x: 2, y: 2, z: 4, core: 2. Of those that a mesh axis runs over, the one named last changes fastest.
Arguments:
- frames: bfloat16 [2, 2048, 1280], P(None, ('dp', 'mp')), may hold values from -8 to 8
- dec_states: bfloat16 [2, 512, 1280], P(None, 'dp'), may hold values from -8 to 8
- out_grad: bfloat16 [2, 512, 1280], P(None, 'dp'), may hold values from -3 to 3
- frame_lengths: int32 [2, 8, 4], P(None, 'dp'), may hold values from 1 to 128, 256 in all within a row
- token_lengths: int32 [2, 8, 4], P(None, 'dp'), may hold values from 1 to 32, 64 in all within a row
- weights: bfloat16 [2, 4, 1024, 1280], P('segment', None, 'mp'), may hold values from -1 to 1
- norm_gains: float32 [3, 1280], replicated, may hold values from 0.25 to 1.75
- norm_biases: float32 [3, 1280], replicated, may hold values from -2 to 2
Outputs:
- gradient: float32 [2, 3, 1024, 1280], P('segment', None, 'mp')
Inputs may be any that keep to these rules, and one draw needn't show every extreme that they name: `frame_lengths`: the 4 utterance lengths of each micro-batch and group sum to 256. `token_lengths`: the 4 token counts of each micro-batch and group sum to 64.
All inputs are finite; a program needn't handle non-finite values.
Results may differ from a plain program's by a relative error of at most 0.04.
Values may be sent and summed in bfloat16 or wider, within the bound.
A program may use at most 64 MiB of HBM per device.

v0:
```python
import math

import jax
import jax.numpy as jnp
from jax import lax
from jax.sharding import PartitionSpec as P

HS = 64


EPSILON = 1e-05
ROWS_DIMS = (((0,), (0,)), ((), ()))
FEAT_DIMS = (((1,), (1,)), ((), ()))


def partner(shard, axis, apart):
    return lax.ppermute(shard, axis, [(i, i ^ 1 << apart) for i in range(lax.axis_size(axis))])


def layer_norm(values, norm_gain, offset):
    center = values - jnp.mean(values, axis=-1, keepdims=True)
    variance = jnp.mean(center * center, axis=-1, keepdims=True)
    return center * lax.rsqrt(variance + EPSILON) * norm_gain + offset


def norm_backward(grad_out, values, norm_gain):
    center = values - jnp.mean(values, axis=-1, keepdims=True)
    variance = jnp.mean(center * center, axis=-1, keepdims=True)
    inverse = lax.rsqrt(variance + EPSILON)
    normed = center * inverse
    scaled = grad_out * norm_gain
    return inverse * (
        scaled
        - jnp.mean(scaled, axis=-1, keepdims=True)
        - normed * jnp.mean(scaled * normed, axis=-1, keepdims=True)
    )


def utterance_ids(lengths, row_count):
    bounds = jnp.cumsum(lengths, axis=1, dtype=jnp.int32)
    places = jnp.arange(row_count, dtype=jnp.int32)
    local_ids = jnp.sum((places[None, :, None] >= bounds[:, None, :]).astype(jnp.int32), axis=2)
    offsets = jnp.arange(lengths.shape[0], dtype=jnp.int32)[:, None] * lengths.shape[1]
    return (local_ids + offsets).reshape(-1)


def project(row_block, matrix):
    return lax.dot_general(row_block, matrix, FEAT_DIMS, preferred_element_type=jnp.float32).astype(
        jnp.bfloat16
    )


def outer_rows(left_rows, right_rows):
    return lax.dot_general(left_rows, right_rows, ROWS_DIMS, preferred_element_type=jnp.float32)


def split_heads(row_block):
    return row_block.reshape(row_block.shape[0], -1, HS)


def attend(queries, key_rows, value_rows, allowed):
    scaling = 1.0 / math.sqrt(HS)
    scores = (
        jnp.einsum(
            "qhd,khd->hqk",
            split_heads(queries),
            split_heads(key_rows),
            preferred_element_type=jnp.float32,
        )
        * scaling
    )
    scores = jnp.where(allowed[None], scores, -1e30)
    highest = jnp.max(scores, axis=-1, keepdims=True)
    raised = jnp.exp(scores - highest)
    attn_probs = raised / jnp.sum(raised, axis=-1, keepdims=True)
    context = jnp.einsum(
        "hqk,khd->qhd",
        attn_probs.astype(jnp.bfloat16),
        split_heads(value_rows),
        preferred_element_type=jnp.float32,
    )
    return (context.reshape(queries.shape[0], -1).astype(jnp.bfloat16), attn_probs)


def attend_backward(queries, key_rows, value_rows, attn_probs, grad_context):
    scaling = 1.0 / math.sqrt(HS)
    grad_heads = split_heads(grad_context)
    grad_probs = jnp.einsum(
        "qhd,khd->hqk", grad_heads, split_heads(value_rows), preferred_element_type=jnp.float32
    )
    grad_scores = (
        attn_probs * (grad_probs - jnp.sum(grad_probs * attn_probs, axis=-1, keepdims=True))
    ).astype(jnp.bfloat16)
    key_grad = (
        jnp.einsum(
            "hqk,qhd->khd", grad_scores, split_heads(queries), preferred_element_type=jnp.float32
        )
        * scaling
    )
    key_grad = key_grad.reshape(key_rows.shape[0], -1).astype(jnp.bfloat16)
    value_grad = jnp.einsum(
        "hqk,qhd->khd",
        attn_probs.astype(jnp.bfloat16),
        grad_heads,
        preferred_element_type=jnp.float32,
    )
    value_grad = value_grad.reshape(key_rows.shape[0], -1).astype(jnp.bfloat16)
    return (key_grad, value_grad)


def shards(
    frames, dec_states, out_grad, frame_lengths, token_lengths, weights, norm_gains, norm_biases
):
    is_encoder = lax.axis_index("segment") == 0
    matrices = weights[0]
    micro_count = frames.shape[0]
    shard_rows = frames.shape[1]
    features = frames.shape[2]
    head_cols = matrices.shape[1]
    head_count = head_cols // HS
    frame_count = shard_rows * lax.axis_size("mp")
    token_count = dec_states.shape[1]
    unit_count = micro_count // micro_count
    unit_rows = micro_count * frame_count
    received = jnp.zeros((micro_count, shard_rows, features), jnp.bfloat16)

    def empty_state():
        return (
            jnp.zeros((unit_rows, features), jnp.bfloat16),
            jnp.zeros((unit_rows, head_cols), jnp.bfloat16),
            jnp.zeros((unit_rows, head_cols), jnp.bfloat16),
            jnp.zeros((unit_rows, head_cols), jnp.bfloat16),
            jnp.zeros((unit_rows, head_cols), jnp.bfloat16),
            jnp.zeros((head_count, unit_rows, unit_rows), jnp.float32),
        )

    stored = {}
    totals = jnp.zeros((3, head_cols, features), jnp.float32)
    for moment in range(unit_count + 2):
        run_enc = moment < unit_count
        run_dec = 1 <= moment <= unit_count
        run_back = moment >= 2
        if run_enc:
            inputs = frames
        else:
            inputs = jnp.zeros((micro_count, shard_rows, features), jnp.bfloat16)
        enc_full, dec_full = (
            lax.all_gather(inputs, "mp", axis=1, tiled=True),
            lax.all_gather(received, "mp", axis=1, tiled=True),
        )

        def encoder_part():
            partial_value = jnp.zeros((unit_rows, features), jnp.float32)
            grad_step = jnp.zeros((3, head_cols, features), jnp.float32)
            saved_state = empty_state()
            if run_enc:
                lengths = frame_lengths[moment * micro_count : (moment + 1) * micro_count, 0]
                frame_ids = utterance_ids(lengths, frame_count)
                row_input = enc_full.reshape(unit_rows, features)
                normed = layer_norm(
                    row_input.astype(jnp.float32), norm_gains[0], norm_biases[0]
                ).astype(jnp.bfloat16)
                queries = project(normed, matrices[0])
                key_rows = project(normed, matrices[1])
                value_rows = project(normed, matrices[2])
                context, attn_probs = attend(
                    queries, key_rows, value_rows, frame_ids[:, None] == frame_ids[None, :]
                )
                partial_value = jnp.dot(context, matrices[3], preferred_element_type=jnp.float32)
                saved_state = (normed, queries, key_rows, value_rows, context, attn_probs)
            if run_back:
                normed_old, queries_old, keys_old, values_old, context_old, probs_old = stored[
                    moment - 2
                ]
                grad_rows = dec_full.reshape(unit_rows, features)
                out_weight_grad = outer_rows(context_old, grad_rows)
                grad_context = project(grad_rows, matrices[3])
                key_grad, value_grad = attend_backward(
                    queries_old, keys_old, values_old, probs_old, grad_context
                )
                grad_step = jnp.stack(
                    [
                        outer_rows(key_grad, normed_old),
                        outer_rows(value_grad, normed_old),
                        out_weight_grad,
                    ]
                )
            return (partial_value, grad_step, saved_state)

        def decoder_part():
            partial_value = jnp.zeros((unit_rows, features), jnp.float32)
            grad_step = jnp.zeros((3, head_cols, features), jnp.float32)
            if run_dec:
                batch_index = moment - 1
                first_micro = batch_index * micro_count
                frame_ids = utterance_ids(
                    frame_lengths[first_micro : first_micro + micro_count, 0], frame_count
                )
                token_ids = utterance_ids(
                    token_lengths[first_micro : first_micro + micro_count, 0], token_count
                )
                tokens = dec_states.reshape(micro_count * token_count, features)
                upstream = out_grad.reshape(micro_count * token_count, features)
                states_in = dec_full.reshape(unit_rows, features)
                normed = layer_norm(
                    states_in.astype(jnp.float32), norm_gains[2], norm_biases[2]
                ).astype(jnp.bfloat16)
                token_normed = layer_norm(
                    tokens.astype(jnp.float32), norm_gains[1], norm_biases[1]
                ).astype(jnp.bfloat16)
                queries = project(token_normed, matrices[0])
                key_rows = project(normed, matrices[1])
                value_rows = project(normed, matrices[2])
                context, attn_probs = attend(
                    queries, key_rows, value_rows, token_ids[:, None] == frame_ids[None, :]
                )
                grad_context = project(upstream, matrices[3])
                out_weight_grad = outer_rows(context, upstream)
                key_grad, value_grad = attend_backward(
                    queries, key_rows, value_rows, attn_probs, grad_context
                )
                grad_step = jnp.stack(
                    [outer_rows(key_grad, normed), outer_rows(value_grad, normed), out_weight_grad]
                )
                partial_value = jnp.dot(
                    key_grad, matrices[1], preferred_element_type=jnp.float32
                ) + jnp.dot(value_grad, matrices[2], preferred_element_type=jnp.float32)
            return (partial_value, grad_step, empty_state())

        partial_value, grad_step, saved_state = lax.cond(is_encoder, encoder_part, decoder_part)
        totals = totals + grad_step
        if run_enc:
            stored[moment] = saved_state
        if run_enc or run_dec:
            partial_value = partial_value.reshape(micro_count, frame_count, features)
            summed = lax.psum_scatter(
                partial_value.astype(jnp.bfloat16), "mp", scatter_dimension=1, tiled=True
            ).astype(jnp.float32)
            states_out = (inputs.astype(jnp.float32) + summed).astype(jnp.bfloat16)
            grads_out = norm_backward(summed, received.astype(jnp.float32), norm_gains[2]).astype(
                jnp.bfloat16
            )
            received = partner(jnp.where(is_encoder, states_out, grads_out), "segment", 0)
    gradient = lax.psum(totals.astype(jnp.bfloat16), "dp").astype(jnp.float32)
    return gradient[None]


def solution(mesh):
    placed = (
        P(None, ("dp", "mp"), None),
        P(None, "dp", None),
        P(None, "dp", None),
        P(None, "dp", None),
        P(None, "dp", None),
        P("segment", None, "mp", None),
        P(),
        P(),
    )
    return jax.shard_map(
        shards,
        mesh=mesh,
        in_specs=placed,
        out_specs=P("segment", None, "mp", None),
        check_vma=False,
    )
```

profile of v0, /device:TPU:0, one launch (start us, length us, event | category | flops | bytes accessed | tf_op | source)
XLA Modules:
  0.0 413.5 jit_solution(17051785579873963105)
XLA Ops:
  6.5 0.7 all-gather.4.cloned.1.call-update
  7.3 0.0 reduce-scatter.3.cloned.1.call-start
  7.3 28.6 %all-gather.4.cloned.1.call-done = bf16[2,256,1280]{2,1,0:T(8,128)(2,1)} async-done(((bf16[2,128,1280]{2,1,0:T(8,128)(2,1)}), bf16[2,256,1280]{2,1,0:T(8,128)(2,1)}) %all-gather.4.cloned.1.call-update) | async-done | bytes 1310736 | tf_op jit(solution)/shard_map/all_gather | solution.py:148
  35.9 30.9 %conditional.3 = (bf16[512,1280]{1,0:T(8,128)(2,1)S(1)}, bf16[512,1280]{1,0:T(8,128)(2,1)}, bf16[512,512]{0,1:T(8,128)(2,1)S(1)}, bf16[512,512]{0,1:T(8,128)(2,1...) conditional(s32[]{:T(128)} %convert_element_type.217, () %tuple.34, ...), branch_computations={%region_0.0_spmd, %region_1.8_spmd} | conditional | flops 3246922752 | bytes 91347304 | solution.py:230
  35.9 1.0 reduce_window_sum.17
  36.8 0.1 convert_reduce_fusion.1
  36.9 0.1 add_bitcast_fusion
  37.0 1.6 convert_reduce_fusion
  38.6 0.5 multiply_reduce_fusion.1
  39.1 0.8 slice_reduce_fusion
  39.9 0.2 broadcast_compare_fusion
  40.1 1.6 fusion.25
  41.8 0.6 add_convert_fusion
  42.3 0.8 copy-done.15
  43.1 0.9 fusion.44
  44.0 0.9 fusion.41
  44.9 0.9 fusion.47
  45.8 5.4 %fusion.131 = (f32[8,512]{1,0:T(8,128)S(1)}, f32[8,512,512]{1,2,0:T(8,128)}) fusion(pred[512,512]{0,1:T(8,128)(4,1)S(1)} %broadcast_compare_fusion, bf16[512,8,64]{0,2,1:T(8,128)(2,1)S(1)} %bitcast.170, bf16[512,8,64]{0,2,1:T(8,128)(2,1)S(1)} %bitcast.209), kind=kOutput, calls=%fused_computation.177 | convolution fusion | flops 276824576 | bytes 9715712 | tf_op jit(solution)/shard_map/cond/branch_1_fun/sub | solution.py:74
  51.2 8.2 %broadcast_divide_fusion = f32[8,512,512]{1,2,0:T(8,128)} fusion(f32[8,512,512]{1,2,0:T(8,128)} %get-tuple-element.194, f32[8,512]{1,0:T(8,128)S(1)} %get-tuple-element.193), kind=kLoop, calls=%fused_computation.23 | loop fusion | flops 2097152 | bytes 16793600 | tf_op jit(solution)/shard_map/cond/branch_1_fun/div | solution.py:75
  59.3 5.0 %fusion.38 = bf16[8,64,512]{2,1,0:T(8,128)(2,1)} fusion(bf16[512,8,64]{0,2,1:T(8,128)(2,1)S(1)} %bitcast.166, f32[8,512,512]{1,2,0:T(8,128)} %broadcast_divide_fusion), kind=kOutput, calls=%fused_computation.47 | convolution fusion | flops 270794752 | bytes 9437184 | tf_op jit(solution)/shard_map/cond/branch_1_fun/hqk,khd->qhd/dot_general | solution.py:76
  64.3 2.4 fusion.26
  66.9 1.0 copy-done.4
  67.9 0.0 reduce-scatter.3.cloned.1.call-update
  67.9 0.0 all-gather.6.cloned.1.call-start
  67.9 0.7 slice_reduce_fusion.6
  68.7 22.5 %reduce-scatter.3.cloned.1.call-done = bf16[2,128,1280]{2,1,0:T(8,128)(2,1)} async-done(((bf16[2,256,1280]{2,1,0:T(8,128)(2,1)}), bf16[2,128,1280]{2,1,0:T(8,128)(2,1)}) %reduce-scatter.3.cloned.1.call-update) | async-done | bytes 655376 | tf_op jit(solution)/shard_map/reduce_scatter | solution.py:236
  91.2 1.4 fusion.113
  92.7 1.5 fusion.130
  94.1 0.1 collective-permute-start
  94.2 2.1 collective-permute-done
  96.3 0.8 copy-done.1
  97.2 0.0 reduce-scatter.5.cloned.1.call-start
  97.2 24.4 %all-gather.6.cloned.1.call-done = bf16[2,256,1280]{2,1,0:T(8,128)(2,1)} async-done(((bf16[2,128,1280]{2,1,0:T(8,128)(2,1)}), bf16[2,256,1280]{2,1,0:T(8,128)(2,1)}) %all-gather.6.cloned.1.call-update) | async-done | bytes 1310736 | tf_op jit(solution)/shard_map/all_gather | solution.py:149
  121.6 4.1 %conditional.4 = (bf16[512,1280]{1,0:T(8,128)(2,1)S(1)}, f32[3,512,1280]{2,1,0:T(8,128)}) conditional(s32[]{:T(128)} %convert_element_type.217, (bf16[2,64,1280]{2,1,0:T(8,128)(2,1)S(1)}, f32[3,1280]{1,0:T(4,128)S(1)}, f32[3,1280]{1,0:T(4,128)S(1)}, bf16[4,512,1280]{2,1,0:T(8,128)(2,1)}, s32[2,1,4]{2,1,0:T(1,128)S(1)}, ...), branch_computations={%region_11.23_spmd, %region_23.24_spmd} | conditional | flops 4889911296 | bytes 113442840 | solution.py:230
  121.8 0.1 broadcast.393
  121.9 3.8 broadcast.394
  125.7 1.2 copy-done.5
  126.9 0.0 reduce-scatter.5.cloned.1.call-update
  126.9 0.0 all-gather.8.cloned.1.call-start
  127.0 0.2 convert_reduce_fusion.6
  127.2 0.3 fusion.122
  127.5 53.4 %reduce-scatter.5.cloned.1.call-done = bf16[2,128,1280]{2,1,0:T(8,128)(2,1)} async-done(((bf16[2,256,1280]{2,1,0:T(8,128)(2,1)}), bf16[2,128,1280]{2,1,0:T(8,128)(2,1)}) %reduce-scatter.5.cloned.1.call-update) | async-done | bytes 655376 | tf_op jit(solution)/shard_map/reduce_scatter | solution.py:236
  180.9 1.5 fusion.128
  182.4 1.9 fusion.129
  184.3 0.1 collective-permute-start.1
  184.4 2.1 collective-permute-done.1
  186.5 0.9 copy-done.16
  187.4 0.0 all-gather.8.cloned.1.call-update
  187.4 0.0 all-reduce.2.cloned.1.call-start
  187.5 24.4 %all-gather.8.cloned.1.call-done = bf16[2,256,1280]{2,1,0:T(8,128)(2,1)} async-done(((bf16[2,128,1280]{2,1,0:T(8,128)(2,1)}), bf16[2,256,1280]{2,1,0:T(8,128)(2,1)}) %all-gather.8.cloned.1.call-update) | async-done | bytes 1310736 | tf_op jit(solution)/shard_map/all_gather | solution.py:149
  211.8 30.8 %conditional.5 = (f32[3,512,1280]{2,1,0:T(8,128)}) conditional(s32[]{:T(128)} %convert_element_type.217, () %tuple.38, (bf16[2,256,1280]{2,1,0:T(8,128)(2,1)}, bf16[4,512,1280]{2,1,0:T(8,128)(2,1)}, bf16[512,512]{0,1:T(8,128)(2,1)S(1)}, f32[8,512,512]{1,2,0:T(8,128)}, bf16[512,512]{0,1:T(8,128)(2,1)S(1)}, /*index=5*/bf16[512,1280]{1,0:T(8,128)(2,1)}, ...), branch_computations={%region_29.30_spmd, %region_30.32_spmd} | conditional | flops 3507220480 | bytes 103579736 | solution.py:230
  211.8 2.6 fusion.11
  214.4 4.9 %fusion.8 = bf16[8,64,512]{2,1,0:T(8,128)(2,1)S(1)} fusion(bf16[512,8,64]{0,2,1:T(8,128)(2,1)S(1)} %bitcast.168, f32[8,512,512]{1,2,0:T(8,128)} %get-tuple-element.88), kind=kOutput, calls=%fused_computation.14 | convolution fusion | flops 270794752 | bytes 9437184 | tf_op jit(solution)/shard_map/cond/branch_1_fun/hqk,qhd->khd/dot_general | solution.py:101
  219.3 3.5 convolution_bitcast_fusion
  222.8 3.7 convolution_bitcast_fusion.1
  226.5 4.7 %multiply_reduce_fusion = (f32[8,512]{1,0:T(8,128)S(1)}, f32[8,512,512]{1,2,0:T(8,128)S(1)}) fusion(f32[8,512,512]{1,2,0:T(8,128)} %get-tuple-element.88, bf16[512,8,64]{0,2,1:T(8,128)(2,1)S(1)} %bitcast.169, bf16[512,8,64]{0,2,1:T(8,128)(2,1)S(1)} %bitcast.167), kind=kOutput, calls=%fused_computation.1 | convolution fusion | flops 272625664 | bytes 17842176 | tf_op jit(solution)/shard_map/cond/branch_1_fun/qhd,khd->hqk/dot_general | solution.py:88
  231.3 5.1 %fusion.14 = bf16[8,512,64]{1,2,0:T(8,128)(2,1)S(1)} fusion(bf16[512,8,64]{0,2,1:T(8,128)(2,1)S(1)} %bitcast.171, f32[8,512,512]{1,2,0:T(8,128)} %get-tuple-element.88, f32[8,512,512]{1,2,0:T(8,128)S(1)} %get-tuple-element.188, f32[8,512]{1,0:T(8,128)S(1)} %get-tuple-element.187), kind=kOutput, calls=%fused_computation.16 | convolution fusion | flops 275251200 | bytes 17842176 | tf_op jit(solution)/shard_map/cond/branch_1_fun/hqk,qhd->khd/dot_general | solution.py:95
  236.3 2.3 convolution_bitcast_fusion.2
  238.7 0.6 copy-done.11
  239.2 3.4 pad_maximum_fusion
  242.6 8.4 %fusion.110 = bf16[1,3,512,1280]{3,2,1,0:T(8,128)(2,1)} fusion(f32[3,512,1280]{2,1,0:T(8,128)} %get-tuple-element.223, f32[3,512,1280]{2,1,0:T(8,128)} %get-tuple-element.106, f32[]{:T(128)} %get-tuple-element.104), kind=kLoop, calls=%fused_computation.144 | loop fusion | flops 5898240 | bytes 19660804 | tf_op jit(solution)/shard_map/broadcast_in_dim | solution.py:245
  251.1 0.0 all-reduce.2.cloned.1.call-update
  251.1 149.5 %all-reduce.2.cloned.1.call-done = bf16[1,3,512,1280]{3,2,1,0:T(8,128)(2,1)} async-done(((bf16[1,3,512,1280]{3,2,1,0:T(8,128)(2,1)}), bf16[1,3,512,1280]{3,2,1,0:T(8,128)(2,1)}) %all-reduce.2.cloned.1.call-update) | async-done | bytes 3932176 | tf_op jit(solution)/shard_map/psum | solution.py:244
  400.6 6.0 %broadcast_in_dim.37 = f32[1,3,512,1280]{3,2,1,0:T(8,128)} convert(bf16[1,3,512,1280]{3,2,1,0:T(8,128)(2,1)} %all-reduce.2.cloned.1.call-done) | non-fusion elementwise | flops 1966080 | bytes 11796480 | tf_op jit(solution)/shard_map/broadcast_in_dim | solution.py:245
  (47 shorter events, 0.2 us)
Async XLA Ops:
  6.5 29.4 %all-gather.4.cloned.1.call-start = ((), (), s32[]{:S(2)}) async-start(), calls=%async_computation.2 | async-start | bytes 1966080 | tf_op jit(solution)/shard_map/all_gather | solution.py:148
  7.3 84.0 %reduce-scatter.3.cloned.1.call-start = ((), (), s32[]{:S(2)}) async-start(), calls=%async_computation.3 | async-start | bytes 1966080 | tf_op jit(solution)/shard_map/reduce_scatter | solution.py:236
  35.9 2.7 copy-start
  40.1 3.0 copy-start.15
  44.0 1.8 copy-start.12
  44.9 14.5 %copy-start.6 = (bf16[512,512]{0,1:T(8,128)(2,1)}, bf16[512,512]{0,1:T(8,128)(2,1)S(1)}, u32[]{:S(2)}) copy-start(bf16[512,512]{0,1:T(8,128)(2,1)S(1)} %fusion.41) | copy-start | bytes 1572868 | tf_op jit(solution)/shard_map/cond
  64.3 2.4 copy-start.7
  64.3 2.4 copy-start.13
  66.8 1.1 copy-start.4
  66.8 25.8 %copy-start.9 = (bf16[2,128,1280]{2,1,0:T(8,128)(2,1)S(1)}, bf16[2,128,1280]{2,1,0:T(8,128)(2,1)}, u32[]{:S(2)}) copy-start(bf16[2,128,1280]{2,1,0:T(8,128)(2,1)} %param.14) | copy-start | bytes 1966084
  66.8 54.7 %copy-start.8 = (bf16[2,64,1280]{2,1,0:T(8,128)(2,1)S(1)}, bf16[2,64,1280]{2,1,0:T(8,128)(2,1)}, u32[]{:S(2)}) copy-start(bf16[2,64,1280]{2,1,0:T(8,128)(2,1)} %param.15) | copy-start | bytes 983044
  66.8 54.7 %copy-start.21 = (f32[3,1280]{1,0:T(4,128)S(1)}, f32[3,1280]{1,0:T(4,128)}, u32[]{:S(2)}) copy-start(f32[3,1280]{1,0:T(4,128)} %param.20) | copy-start | bytes 46084
  66.9 54.7 %copy-start.22 = (f32[3,1280]{1,0:T(4,128)S(1)}, f32[3,1280]{1,0:T(4,128)}, u32[]{:S(2)}) copy-start(f32[3,1280]{1,0:T(4,128)} %param.21) | copy-start | bytes 46084
  66.9 54.7 %copy-start.24 = (s32[2,1,4]{2,1,0:T(1,128)S(1)}, s32[2,1,4]{2,1,0:T(1,128)}, u32[]{:S(2)}) copy-start(s32[2,1,4]{2,1,0:T(1,128)} %param.17) | copy-start | bytes 100
  66.9 54.7 %copy-start.25 = (s32[2,1,4]{2,1,0:T(1,128)S(1)}, s32[2,1,4]{2,1,0:T(1,128)}, u32[]{:S(2)}) copy-start(s32[2,1,4]{2,1,0:T(1,128)} %param.18) | copy-start | bytes 100
  67.9 53.7 %all-gather.6.cloned.1.call-start = ((), (), s32[]{:S(2)}) async-start(), calls=%async_computation.4 | async-start | bytes 1966080 | tf_op jit(solution)/shard_map/all_gather | solution.py:149
  94.1 2.2 collective-permute-start
  96.3 0.8 copy-start.1
  97.2 83.8 %reduce-scatter.5.cloned.1.call-start = ((), (), s32[]{:S(2)}) async-start(), calls=%async_computation.5 | async-start | bytes 1966080 | tf_op jit(solution)/shard_map/reduce_scatter | solution.py:236
  121.6 5.4 %copy-start.2 = (bf16[2,128,1280]{2,1,0:T(8,128)(2,1)S(1)}, bf16[2,128,1280]{2,1,0:T(8,128)(2,1)}, u32[]{:S(2)}) copy-start(bf16[2,128,1280]{2,1,0:T(8,128)(2,1)} %copy-done.1) | copy-start | bytes 1966084
  125.7 1.2 copy-start.5
  126.9 84.9 %all-gather.8.cloned.1.call-start = ((), (), s32[]{:S(2)}) async-start(), calls=%async_computation.6 | async-start | bytes 1966080 | tf_op jit(solution)/shard_map/all_gather | solution.py:149
  184.3 2.2 collective-permute-start.1
  186.5 0.9 copy-start.16
  187.4 213.2 %all-reduce.2.cloned.1.call-start = ((), (), s32[]{:S(2)}) async-start(), calls=%async_computation.7 | async-start | bytes 7864320 | tf_op jit(solution)/shard_map/psum | solution.py:244
  214.4 4.9 %copy-start.26 = (bf16[2,256,1280]{2,1,0:T(8,128)(2,1)S(1)}, bf16[2,256,1280]{2,1,0:T(8,128)(2,1)}, u32[]{:S(2)}) copy-start(bf16[2,256,1280]{2,1,0:T(8,128)(2,1)} %get-tuple-element.89) | copy-start | bytes 3932164 | tf_op jit(solution)/shard_map/cond
  236.3 2.3 copy-start.10
  236.3 2.9 copy-start.11
Sparse Core Ops, SparseCore 0:
  8.9 26.9 all-gather.3
  68.0 23.1 reduce-scatter.2
  97.3 24.2 all-gather.5
  127.0 53.8 reduce-scatter.4
  187.5 24.2 all-gather.7
  251.2 149.3 all-reduce.1
where the time goes:
time: 414 us; the launch traced here: 413 us
  waiting for transfers between devices  308 us (74%)
  matrix products  42.2 us (10%)
  other arithmetic  38.3 us (9%)
  between operations  13.6 us (3%)
  local copies, waits for them, and re-layouts  10.8 us (3%)
    psum x1, waiting for transfers between devices, shards(): gradient = lax.psum(totals.astype(jnp.bfloat16), 'dp').astype(jnp.float32)  150 us
    reduce_scatter x2, waiting for transfers between devices, shards(): lax.psum_scatter(partial_value.astype(jnp.bfloat16), 'mp', scatter_dimens...  76 us
    all_gather x2, waiting for transfers between devices, shards(): lax.all_gather(received, 'mp', axis=1, tiled=True)  48.7 us
    all_gather x1, waiting for transfers between devices, shards(): lax.all_gather(inputs, 'mp', axis=1, tiled=True)  28.6 us
    broadcast_in_dim x2, other arithmetic, shards(): return gradient[None]  14.4 us
    dot_general x3, matrix products, outer_rows(): lax.dot_general(left_rows, right_rows, ROWS_DIMS, preferred_element_type=...  9.52 us
  transfers between devices with their start and end apart: 8, of which 8 were waited for; matrix products, arithmetic and copies ran while one was open for 0% of the time, Pallas kernels for 0%

commit v1 on v0

v1 whole, which is shorter than its diff:
```python
import functools
import math

import jax
import jax.numpy as jnp
from jax import lax
from jax.experimental import pallas as pl
from jax.experimental.pallas import tpu as pltpu
from jax.sharding import PartitionSpec as P

HS = 64
EPSILON = 1e-05
MESH = pl.DeviceIdType.MESH
F32 = jnp.float32
BF16 = jnp.bfloat16
NEAR = 2
CHUNKS = 4


def layer_norm(values, norm_gain, offset):
    center = values - jnp.mean(values, axis=-1, keepdims=True)
    variance = jnp.mean(center * center, axis=-1, keepdims=True)
    return center * lax.rsqrt(variance + EPSILON) * norm_gain + offset


def norm_backward(grad_out, values, norm_gain):
    center = values - jnp.mean(values, axis=-1, keepdims=True)
    variance = jnp.mean(center * center, axis=-1, keepdims=True)
    inverse = lax.rsqrt(variance + EPSILON)
    normed = center * inverse
    scaled = grad_out * norm_gain
    return inverse * (
        scaled
        - jnp.mean(scaled, axis=-1, keepdims=True)
        - normed * jnp.mean(scaled * normed, axis=-1, keepdims=True)
    )


def utterance_ids(lengths, row_count):
    bounds = jnp.cumsum(lengths, dtype=jnp.int32)
    places = jnp.arange(row_count, dtype=jnp.int32)
    return jnp.sum((places[:, None] >= bounds[None, :]).astype(jnp.int32), axis=1)


def project(row_block, matrix):
    return lax.dot_general(
        row_block, matrix, (((1,), (1,)), ((), ())), preferred_element_type=F32
    ).astype(BF16)


def outer_rows(left_rows, right_rows):
    return lax.dot_general(
        left_rows, right_rows, (((0,), (0,)), ((), ())), preferred_element_type=F32
    )


def split_heads(row_block):
    return row_block.reshape(row_block.shape[0], -1, HS)


def attend(queries, key_rows, value_rows, allowed):
    scaling = 1.0 / math.sqrt(HS)
    scores = (
        jnp.einsum(
            "qhd,khd->hqk", split_heads(queries), split_heads(key_rows), preferred_element_type=F32
        )
        * scaling
    )
    scores = jnp.where(allowed[None], scores, -1e30)
    highest = jnp.max(scores, axis=-1, keepdims=True)
    raised = jnp.exp(scores - highest)
    probs = raised * (1.0 / jnp.sum(raised, axis=-1, keepdims=True))
    probs = probs.astype(BF16)
    context = jnp.einsum("hqk,khd->qhd", probs, split_heads(value_rows), preferred_element_type=F32)
    return (context.reshape(queries.shape[0], -1).astype(BF16), probs)


def attend_backward(queries, value_rows, probs, grad_context):
    scaling = 1.0 / math.sqrt(HS)
    grad_heads = split_heads(grad_context)
    row_count = value_rows.shape[0]
    grad_probs = jnp.einsum(
        "qhd,khd->hqk", grad_heads, split_heads(value_rows), preferred_element_type=F32
    )
    wide = probs.astype(F32)
    grad_scores = (
        wide * (grad_probs - jnp.sum(grad_probs * wide, axis=-1, keepdims=True))
    ).astype(BF16)
    key_grad = (
        jnp.einsum("hqk,qhd->khd", grad_scores, split_heads(queries), preferred_element_type=F32)
        * scaling
    )
    value_grad = jnp.einsum("hqk,qhd->khd", probs, grad_heads, preferred_element_type=F32)
    return (
        key_grad.reshape(row_count, -1).astype(BF16),
        value_grad.reshape(row_count, -1).astype(BF16),
    )


def sum_kernel(
    near, far, chunks, g_ref, out_ref, near_in, held, far_in,
    near_send, near_recv, far_send, far_recv, back_send, back_recv, last_send, last_recv,
):
    me = lax.axis_index("dp")
    b = lax.rem(me, near)
    a = lax.div(me, near)
    other = a * near + (1 - b)

    def far_peer(apart):
        return lax.rem(a + apart, far) * near + b

    barrier = pltpu.get_barrier_semaphore()
    pl.semaphore_signal(barrier, inc=1, device_id={"dp": other}, device_id_type=MESH)
    for apart in range(1, far):
        pl.semaphore_signal(barrier, inc=1, device_id={"dp": far_peer(apart)}, device_id_type=MESH)
    pl.semaphore_wait(barrier, far)

    def near_copy(k):
        return pltpu.make_async_remote_copy(
            src_ref=g_ref.at[k, 1 - b],
            dst_ref=near_in.at[k],
            send_sem=near_send.at[k],
            recv_sem=near_recv.at[k],
            device_id={"dp": other},
            device_id_type=MESH,
        )

    def far_copy(k, apart):
        return pltpu.make_async_remote_copy(
            src_ref=held.at[k, lax.rem(a + apart, far)],
            dst_ref=far_in.at[k, apart - 1],
            send_sem=far_send.at[k, apart - 1],
            recv_sem=far_recv.at[k, apart - 1],
            device_id={"dp": far_peer(apart)},
            device_id_type=MESH,
        )

    def back_copy(k, apart):
        return pltpu.make_async_remote_copy(
            src_ref=out_ref.at[k, b, a],
            dst_ref=out_ref.at[k, b, a],
            send_sem=back_send.at[k, apart - 1],
            recv_sem=back_recv.at[k, apart - 1],
            device_id={"dp": far_peer(apart)},
            device_id_type=MESH,
        )

    def last_copy(k):
        return pltpu.make_async_remote_copy(
            src_ref=out_ref.at[k, b],
            dst_ref=out_ref.at[k, b],
            send_sem=last_send.at[k],
            recv_sem=last_recv.at[k],
            device_id={"dp": other},
            device_id_type=MESH,
        )

    def step_far(k):
        near_copy(k).wait_recv()
        held[k] = (g_ref[k, b].astype(F32) + near_in[k].astype(F32)).astype(BF16)
        for apart in range(1, far):
            far_copy(k, apart).start()

    def step_back(k):
        total = held[k, a].astype(F32)
        for apart in range(1, far):
            far_copy(k, apart).wait_recv()
            total = total + far_in[k, apart - 1].astype(F32)
        out_ref[k, b, a] = total.astype(BF16)
        for apart in range(1, far):
            back_copy(k, apart).start()

    def step_last(k):
        for apart in range(1, far):
            back_copy(k, apart).wait_recv()
        last_copy(k).start()

    for k in range(chunks):
        near_copy(k).start()
    for tick in range(chunks + 2):
        if tick < chunks:
            step_far(tick)
        if 0 <= tick - 1 < chunks:
            step_back(tick - 1)
        if 0 <= tick - 2 < chunks:
            step_last(tick - 2)
    for k in range(chunks):
        last_copy(k).wait_recv()
        near_copy(k).wait_send()
        last_copy(k).wait_send()
        for apart in range(1, far):
            far_copy(k, apart).wait_send()
            back_copy(k, apart).wait_send()


def sum_over_groups(terms):
    near = NEAR
    far = lax.axis_size("dp") // near
    rows, features = terms.shape
    unit = CHUNKS * near * far * 16
    padded = -(-rows // unit) * unit
    if padded != rows:
        terms = jnp.pad(terms, ((0, padded - rows), (0, 0)))
    piece = padded // (CHUNKS * near * far)
    blocks = terms.reshape(CHUNKS, near, far, piece, features)
    dma = pltpu.SemaphoreType.DMA
    out = pl.pallas_call(
        functools.partial(sum_kernel, near, far, CHUNKS),
        out_shape=jax.ShapeDtypeStruct(blocks.shape, BF16),
        in_specs=[pl.BlockSpec(memory_space=pltpu.VMEM)],
        out_specs=pl.BlockSpec(memory_space=pltpu.VMEM),
        scratch_shapes=[
            pltpu.VMEM((CHUNKS, far, piece, features), BF16),
            pltpu.VMEM((CHUNKS, far, piece, features), BF16),
            pltpu.VMEM((CHUNKS, far - 1, piece, features), BF16),
            dma((CHUNKS,)),
            dma((CHUNKS,)),
            dma((CHUNKS, far - 1)),
            dma((CHUNKS, far - 1)),
            dma((CHUNKS, far - 1)),
            dma((CHUNKS, far - 1)),
            dma((CHUNKS,)),
            dma((CHUNKS,)),
        ],
        compiler_params=pltpu.CompilerParams(
            collective_id=0, has_side_effects=True, vmem_limit_bytes=40 * 1024 * 1024
        ),
    )(blocks)
    return out.reshape(padded, features)[:rows]


def hop(values, source, target, apart):
    parts = lax.axis_size("mp")
    pairs = [(source * parts + i, target * parts + (i + apart) % parts) for i in range(parts)]
    return lax.ppermute(values, ("segment", "mp"), pairs)


def shards(
    frames, dec_states, out_grad, frame_lengths, token_lengths, weights, norm_gains, norm_biases
):
    is_encoder = lax.axis_index("segment") == 0
    matrices = weights[0]
    micro_count, shard_rows, features = frames.shape
    head_cols = matrices.shape[1]
    parts = lax.axis_size("mp")
    place = lax.axis_index("mp")
    frame_count = shard_rows * parts
    token_count = dec_states.shape[1]
    micros = range(micro_count)

    inputs = []
    for m in micros:
        full = jnp.zeros((frame_count, features), BF16)
        for apart in range(parts):
            if apart == 0:
                block = frames[m]
            else:
                block = hop(frames[m], 0, 0, apart)
                block = jnp.where(is_encoder, block, hop(block, 0, 1, 0))
            start = ((place - apart) % parts) * shard_rows
            full = lax.dynamic_update_slice(full, block, (start, 0))
        inputs.append(full)

    frame_ids = [utterance_ids(frame_lengths[m, 0], frame_count) for m in micros]
    token_ids = [utterance_ids(token_lengths[m, 0], token_count) for m in micros]

    enc = []
    sums = []
    for m in micros:
        normed = layer_norm(inputs[m].astype(F32), norm_gains[0], norm_biases[0]).astype(BF16)
        queries, key_rows, value_rows = [project(normed, matrices[i]) for i in range(3)]
        context, probs = attend(
            queries, key_rows, value_rows, frame_ids[m][:, None] == frame_ids[m][None, :]
        )
        partial = jnp.dot(context, matrices[3], preferred_element_type=F32).astype(BF16)
        enc.append((normed, queries, value_rows, context, probs))
        pieces = [hop(partial, 0, 1, apart) for apart in range(parts)]
        total = pieces[0].astype(F32)
        for apart in range(1, parts):
            total = total + pieces[apart].astype(F32)
        sums.append((inputs[m].astype(F32) + total).astype(BF16))

    upstream = out_grad.reshape(micro_count * token_count, features)
    tokens = dec_states.reshape(micro_count * token_count, features)
    token_normed = layer_norm(tokens.astype(F32), norm_gains[1], norm_biases[1]).astype(BF16)
    dec_queries = project(token_normed, matrices[0])
    grad_context = project(upstream, matrices[3])
    states = [hop(rows, 1, 0, 0) for rows in sums]
    dec = []
    backs = []
    for m in micros:
        rows = slice(m * token_count, (m + 1) * token_count)
        normed = layer_norm(sums[m].astype(F32), norm_gains[2], norm_biases[2]).astype(BF16)
        key_rows, value_rows = [project(normed, matrices[i]) for i in (1, 2)]
        context, probs = attend(
            dec_queries[rows], key_rows, value_rows, token_ids[m][:, None] == frame_ids[m][None, :]
        )
        key_grad, value_grad = attend_backward(
            dec_queries[rows], value_rows, probs, grad_context[rows]
        )
        partial = (
            jnp.dot(key_grad, matrices[1], preferred_element_type=F32)
            + jnp.dot(value_grad, matrices[2], preferred_element_type=F32)
        ).astype(BF16)
        dec.append((normed, key_grad, value_grad, context))
        total = hop(partial, 1, 0, 0).astype(F32)
        for apart in range(1, parts):
            total = total + hop(partial, 1, 0, apart).astype(F32)
        backs.append(total)

    def joined(items, index):
        return jnp.concatenate([item[index] for item in items], axis=0)

    dec_normed = joined(dec, 0)
    dec_terms = jnp.concatenate(
        [
            outer_rows(joined(dec, 1), dec_normed).astype(BF16),
            outer_rows(joined(dec, 2), dec_normed).astype(BF16),
            outer_rows(joined(dec, 3), upstream).astype(BF16),
        ],
        axis=0,
    )

    def encoder_back():
        grads = []
        state_grads = []
        for m in micros:
            _, queries, value_rows, _, probs = enc[m]
            state_grad = norm_backward(backs[m], states[m].astype(F32), norm_gains[2]).astype(BF16)
            state_grads.append(state_grad)
            grads.append(
                attend_backward(queries, value_rows, probs, project(state_grad, matrices[3]))
            )
        normed = joined(enc, 0)
        return jnp.concatenate(
            [
                outer_rows(joined(grads, 0), normed).astype(BF16),
                outer_rows(joined(grads, 1), normed).astype(BF16),
                outer_rows(joined(enc, 3), jnp.concatenate(state_grads, axis=0)).astype(BF16),
            ],
            axis=0,
        )

    terms = lax.cond(is_encoder, encoder_back, lambda: dec_terms)
    gradient = sum_over_groups(terms).astype(F32)
    return gradient.reshape(1, 3, head_cols, features)


def solution(mesh):
    placed = (
        P(None, ("dp", "mp"), None),
        P(None, "dp", None),
        P(None, "dp", None),
        P(None, "dp", None),
        P(None, "dp", None),
        P("segment", None, "mp", None),
        P(),
        P(),
    )
    return jax.shard_map(
        shards,
        mesh=mesh,
        in_specs=placed,
        out_specs=P("segment", None, "mp", None),
        check_vma=False,
    )
```

time: 414 us -> 244 us (0.59)
  waiting for transfers between devices: 308 us -> 5.85 us
  Pallas kernels: 0 us -> 77 us
  starting transfers between devices: 0.35 us -> 25.4 us
  matrix products: 42.2 us -> 63.5 us
  local copies, waits for them, and re-layouts: 10.8 us -> 27.7 us
  between operations: 13.6 us -> 1 us
    psum x1 -> x0, waiting for transfers between devices: 150 us -> none  [shards(): gradient = lax.psum(totals.astype(jnp.bfloat16), 'dp').astype(jnp.float32)]
    all_gather x3 -> x0, waiting for transfers between devices: 77.3 us -> none  [the longest x2 48.7 us: shards(): lax.all_gather(received, 'mp', axis=1, tiled=True)]
    pallas_call x0 -> x1, Pallas kernels: none -> 77 us  [sum_over_groups(): pl.pallas_call(functools.partial(sum_kernel, near, far, CHUNKS), out_shap...]
    reduce_scatter x2 -> x0, waiting for transfers between devices: 76 us -> none  [shards(): lax.psum_scatter(partial_value.astype(jnp.bfloat16), 'mp', scatter_dimens...]
    ppermute x2 -> x14, starting transfers between devices: 0.14 us -> 25.4 us  [hop(): return lax.ppermute(values, ('segment', 'mp'), pairs)]
    dot_general x10 -> x34, matrix products: 27.1 us -> 48.3 us  [the longest x14 25.6 us: project(): lax.dot_general(row_block, matrix, (((1,), (1,)), ((), ())), preferred_el...]
    convert_element_type x2 -> x12, other arithmetic: 2.18 us -> 17.8 us  [the longest x1 3.88 us: shards(): gradient = sum_over_groups(terms).astype(F32)]
    broadcast_in_dim x2 -> x0, other arithmetic: 14.4 us -> none  [shards(): return gradient[None]]
  transfers between devices with their start and end apart: 8 -> 14, of which waited for: 8 -> 3; matrix products, arithmetic and copies ran while one was open for 0% -> 29% of each run, Pallas kernels for 0% -> 0%
where the time goes in v1:
time: 244 us; the launch traced here: 242 us
  Pallas kernels  77 us (32%)
  matrix products  63.5 us (26%)
  other arithmetic  41.7 us (17%)
  local copies, waits for them, and re-layouts  27.7 us (11%)
  starting transfers between devices  25.4 us (10%)
  waiting for transfers between devices  5.85 us (2%)
    pallas_call x1, Pallas kernels, sum_over_groups(): pl.pallas_call(functools.partial(sum_kernel, near, far, CHUNKS), out_shap...  77 us
    dot_general x14, matrix products, project(): lax.dot_general(row_block, matrix, (((1,), (1,)), ((), ())), preferred_el...  25.6 us
    ppermute x14, starting transfers between devices, hop(): return lax.ppermute(values, ('segment', 'mp'), pairs)  25.4 us
    convert_element_type x12, local copies, waits for them, and re-layouts, project(): return lax.dot_general(row_block, matrix, (((1,), (1,)), ((), ())), prefe...  9.89 us
    sub x4, matrix products, attend(): raised = jnp.exp(scores - highest)  8.61 us
    another operation x8, local copies, waits for them, and re-layouts  7.34 us
    dot_general x6, matrix products, outer_rows(): lax.dot_general(left_rows, right_rows, (((0,), (0,)), ((), ())), preferre...  7.11 us
    ppermute x14, waiting for transfers between devices, hop(): return lax.ppermute(values, ('segment', 'mp'), pairs)  5.85 us
  transfers between devices with their start and end apart: 14, of which 3 were waited for; matrix products, arithmetic and copies ran while one was open for 29% of the time, Pallas kernels for 0%

profile of v1, /device:TPU:0, one launch (start us, length us, event | category | flops | bytes accessed | tf_op | source)
XLA Modules:
  0.0 242.4 jit_solution(10718675688877867717)
XLA Ops:
  1.2 4.9 %collective-permute-start = (bf16[128,1280]{1,0:T(8,128)(2,1)S(1)}, bf16[128,1280]{1,0:T(8,128)(2,1)}, u32[]{:S(2)}, u32[]{:S(2)}) collective-permute-start(bf16[128,1280]{1,0:T(8,128)(2,1)S(1)} %get-tuple-element.153), channel_id=1, source_target_pairs={{0,1},{1,0},{4,5},{5,4},{8,9},{9,8},{12,13},{13,12},{16,17},{17,16... | collective-permute-start | bytes 983048 | tf_op jit(solution)/shard_map/ppermute | solution.py:235
  6.1 1.9 collective-permute-start.4
  10.2 1.9 fusion.162
  13.1 1.9 fusion.159
  15.4 1.3 collective-permute-start.1
  20.6 1.3 collective-permute-start.5
  23.6 1.6 select_dynamic-update-slice_fusion
  26.3 2.3 fusion.130
  28.6 1.9 fusion.139
  30.6 1.3 fusion.127
  34.1 2.2 fusion.236
  36.3 1.8 multiply_convert_fusion
  38.4 2.8 %convolution_convert_fusion.8 = bf16[256,1280]{1,0:T(8,128)(2,1)} fusion(bf16[256,512]{0,1:T(8,128)(2,1)S(1)} %bitcast.266, bf16[1,4,512,1280]{3,2,1,0:T(8,128)(2,1)} %param.15), kind=kOutput, calls=%fused_computation.90 | convolution fusion | flops 335872000 | bytes 2228224 | tf_op jit(solution)/shard_map/dot_general | solution.py:275
  41.2 3.0 %collective-permute-start.7 = (bf16[256,1280]{1,0:T(8,128)(2,1)}, bf16[256,1280]{1,0:T(8,128)(2,1)}, u32[]{:S(2)}, u32[]{:S(2)}) collective-permute-start(bf16[256,1280]{1,0:T(8,128)(2,1)} %convolution_convert_fusion.8), channel_id=1, source_target_pairs={{0,3},{1,2},{4,7},{5,6},{8,11},{9,10},{12,15},{13,14},{16,19},{17,... | collective-permute-start | bytes 1966088 | tf_op jit(solution)/shard_map/ppermute | solution.py:235
  44.2 2.1 collective-permute-start.6
  46.7 2.2 fusion.235
  48.8 1.8 multiply_convert_fusion.1
  50.7 1.9 fusion.133
  54.7 1.9 convolution_convert_fusion.9
  56.6 1.5 collective-permute-start.3
  58.1 1.3 collective-permute-start.2
  59.5 2.4 convert_reduce_fusion.4
  61.9 1.5 collective-permute-start.11
  63.3 1.4 fusion.79
  64.8 1.4 collective-permute-done.3
  67.3 1.4 fusion.83
  68.7 2.0 fusion.86
  70.7 3.0 %fusion.136 = bf16[256,512]{1,0:T(8,128)(2,1)} fusion(bf16[256,1280]{1,0:T(8,128)(2,1)S(1)} %get-tuple-element.159, bf16[1,4,512,1280]{3,2,1,0:T(8,128)(2,1)} %param.15), kind=kOutput, calls=%fused_computation.184 | convolution fusion | flops 335675392 | bytes 2228224 | tf_op jit(solution)/shard_map/dot_general | solution.py:46
  73.8 2.6 %fusion.148 = bf16[256,512]{1,0:T(8,128)(2,1)} fusion(bf16[256,1280]{1,0:T(8,128)(2,1)S(1)} %get-tuple-element.159, bf16[1,4,512,1280]{3,2,1,0:T(8,128)(2,1)} %param.15), kind=kOutput, calls=%fused_computation.188 | convolution fusion | flops 335675392 | bytes 2228224 | tf_op jit(solution)/shard_map/dot_general | solution.py:46
  77.6 1.3 fusion.154
  78.8 1.8 copy.96
  80.6 1.8 copy.94
  82.4 2.1 fusion.237
  84.5 2.3 fusion.197
  88.7 1.3 collective-permute-start.8
  90.0 1.8 copy.87
  91.8 1.8 copy.85
  93.6 2.2 fusion.238
  95.8 1.6 fusion.195
  97.9 1.9 fusion.95
  99.9 1.9 fusion.59
  101.8 1.3 collective-permute-start.10
  103.1 1.3 collective-permute-start.9
  107.8 1.4 collective-permute-start.13
  110.9 3.1 %collective-permute-done.10 = bf16[256,1280]{1,0:T(8,128)(2,1)S(1)} collective-permute-done((bf16[256,1280]{1,0:T(8,128)(2,1)S(1)}, bf16[256,1280]{1,0:T(8,128)(2,1)S(1)}, u32[]{:S(2)}, u32[]{:S(2)}) %collective-permute-start.10) | collective-permute-done | bytes 655392 | tf_op jit(solution)/shard_map/ppermute | solution.py:235
  114.1 1.3 collective-permute-start.12
  115.4 2.1 pad_maximum_fusion.1
  119.8 1.3 collective-permute-done.13
  122.3 1.3 convert_element_type.411
  123.5 37.9 %conditional.1 = (bf16[1536,1280]{1,0:T(8,128)(2,1)}) conditional(s32[]{:T(128)} %convert_element_type.338, bf16[1536,1280]{1,0:T(8,128)(2,1)} %pad_maximum_fusion.1, (bf16[8,256,256]{1,2,0:T(8,128)(2,1)S(1)}, bf16[256,1280]{1,0:T(8,128)(2,1)}, f32[256,1280]{1,0:T(8,128)}, f32[256,1280]{1,0:T(8,128)}, f32[3,1280]{1,0:T(4,128)}, ...), branch_computations={%region_28.29_spmd, %region_29.40_spmd} | conditional | flops 3129340416 | bytes 92362080 | solution.py:344
  123.5 1.5 convert_reduce_fusion
  125.1 1.4 fusion.21
  127.6 2.8 %fusion.229 = (f32[256]{0:T(256)S(1)}, f32[256]{0:T(256)S(1)}, f32[256,1280]{1,0:T(8,128)S(1)}, f32[256]{0:T(256)S(1)}, f32[256]{0:T(256)S(1)}, /*index=5*/f32[256,1280]{1,0:T(8,128)S(1)}) fusion(f32[256]{0:T(256)S(1)} %add_rsqrt_fusion.1, f32[256]{0:T(256)S(1)} %broadcast_multiply_fusion.5, bf16[256,1280]{1,0:T(8,128)(2,1)} %get-tuple-element.53, ...), kind=kLoop, calls=%fused_computation.309 | loop fusion | flops 5241856 | bytes 9188352 | tf_op jit(solution)/shard_map/cond/branch_1_fun/reduce_sum | solution.py:34
  130.4 2.3 fusion.15
  134.0 1.9 fusion.34
  136.1 3.2 %convolution_convert_fusion = bf16[512,1280]{1,0:T(8,128)(2,1)} fusion(bf16[256,1280]{1,0:T(8,128)(2,1)} %copy-done.31, bf16[256,1280]{1,0:T(8,128)(2,1)S(1)} %copy-done.30, bf16[256,512]{0,1:T(8,128)(2,1)} %bitcast.267, bf16[256,512]{0,1:T(8,128)(2,1)} %bitcast.269), kind=kOutput, calls=%fused_computation.1 | convolution fusion | flops 675414016 | bytes 3145728 | tf_op jit(solution)/shard_map/cond/branch_1_fun/dot_general | solution.py:52
  139.3 2.6 %fusion.31 = bf16[256,512]{1,0:T(8,128)(2,1)} fusion(bf16[256,1280]{1,0:T(8,128)(2,1)S(1)} %copy-done.30, bf16[1,4,512,1280]{3,2,1,0:T(8,128)(2,1)} %get-tuple-element.57), kind=kOutput, calls=%fused_computation.47 | convolution fusion | flops 335675392 | bytes 2228224 | tf_op jit(solution)/shard_map/cond/branch_1_fun/dot_general | solution.py:46
  145.2 1.9 copy.104
  147.1 1.8 copy.103
  148.9 1.8 copy.102
  150.7 1.8 copy.101
  159.4 2.1 pad_maximum_fusion
  161.5 77.0 %shard_map.82 = bf16[4,2,4,48,1280]{4,3,2,1,0:T(8,128)(2,1)S(1)} custom-call(bf16[4,2,4,48,1280]{4,3,2,1,0:T(8,128)(2,1)} %bitcast.218), custom_call_target="tpu_custom_call" | custom-call | tf_op jit(solution)/shard_map/pallas_call | solution.py:207
  238.5 3.9 %convert.1 = f32[1,3,512,1280]{3,2,1,0:T(8,128)} convert(bf16[1,3,512,1280]{3,2,1,0:T(8,128)(2,1)S(1)} %bitcast.217) | non-fusion elementwise | flops 1966080 | bytes 11796480 | tf_op jit(solution)/shard_map/convert_element_type | solution.py:345
  (224 shorter events, 41.9 us)
Async XLA Ops:
  0.0 10.2 %copy-start = (bf16[2,64,1280]{2,1,0:T(8,128)(2,1)S(1)}, bf16[2,64,1280]{2,1,0:T(8,128)(2,1)}, u32[]{:S(2)}) copy-start(bf16[2,64,1280]{2,1,0:T(8,128)(2,1)} %param.12) | copy-start | bytes 983044
  0.0 8.0 %copy-start.6 = (bf16[2,64,1280]{2,1,0:T(8,128)(2,1)S(1)}, bf16[2,64,1280]{2,1,0:T(8,128)(2,1)}, u32[]{:S(2)}) copy-start(bf16[2,64,1280]{2,1,0:T(8,128)(2,1)} %param.11) | copy-start | bytes 983044
  0.0 8.4 %copy-start.48 = (s32[2,1,4]{2,1,0:T(1,128)S(1)}, s32[2,1,4]{2,1,0:T(1,128)}, u32[]{:S(2)}) copy-start(s32[2,1,4]{2,1,0:T(1,128)} %param.13) | copy-start | bytes 100
  0.0 9.0 %copy-start.49 = (s32[2,1,4]{2,1,0:T(1,128)S(1)}, s32[2,1,4]{2,1,0:T(1,128)}, u32[]{:S(2)}) copy-start(s32[2,1,4]{2,1,0:T(1,128)} %param.14) | copy-start | bytes 100
  1.2 14.2 %collective-permute-start = (bf16[128,1280]{1,0:T(8,128)(2,1)S(1)}, bf16[128,1280]{1,0:T(8,128)(2,1)}, u32[]{:S(2)}, u32[]{:S(2)}) collective-permute-start(bf16[128,1280]{1,0:T(8,128)(2,1)S(1)} %get-tuple-element.153), channel_id=1, source_target_pairs={{0,1},{1,0},{4,5},{5,4},{8,9},{9,8},{12,13},{13,12},{16,17},{17,16... | collective-permute-start | bytes 983048 | tf_op jit(solution)/shard_map/ppermute | solution.py:235
  6.1 14.6 %collective-permute-start.4 = (bf16[128,1280]{1,0:T(8,128)(2,1)S(1)}, bf16[128,1280]{1,0:T(8,128)(2,1)}, u32[]{:S(2)}, u32[]{:S(2)}) collective-permute-start(bf16[128,1280]{1,0:T(8,128)(2,1)S(1)} %get-tuple-element.154), channel_id=1, source_target_pairs={{0,1},{1,0},{4,5},{5,4},{8,9},{9,8},{12,13},{13,12},{16,17},{17,16... | collective-permute-start | bytes 983048 | tf_op jit(solution)/shard_map/ppermute | solution.py:235
  8.2 4.0 %copy-start.43 = (f32[3,1280]{1,0:T(4,128)S(1)}, f32[3,1280]{1,0:T(4,128)}, u32[]{:S(2)}) copy-start(f32[3,1280]{1,0:T(4,128)} %param.16) | copy-start | bytes 46084
  8.2 4.0 %copy-start.46 = (f32[3,1280]{1,0:T(4,128)S(1)}, f32[3,1280]{1,0:T(4,128)}, u32[]{:S(2)}) copy-start(f32[3,1280]{1,0:T(4,128)} %param.17) | copy-start | bytes 46084
  8.7 8.0 %copy-start.47 = (s32[256]{0:T(256)}, s32[256]{0:T(256)S(1)}, u32[]{:S(2)}) copy-start(s32[256]{0:T(256)S(1)} %convert_reduce_fusion.8) | copy-start | bytes 3076
  13.1 2.0 copy-start.11
  15.4 6.6 %collective-permute-start.1 = (bf16[128,1280]{1,0:T(8,128)(2,1)}, bf16[128,1280]{1,0:T(8,128)(2,1)S(1)}, u32[]{:S(2)}, u32[]{:S(2)}) collective-permute-start(bf16[128,1280]{1,0:T(8,128)(2,1)} %collective-permute-done), channel_id=1, source_target_pairs={{0,2},{1,3},{4,6},{5,7},{8,10},{9,11},{12,14},{13,15},{16,18},{17,... | collective-permute-start | bytes 983048 | tf_op jit(solution)/shard_map/ppermute | solution.py:235
  20.6 2.9 %collective-permute-start.5 = (bf16[128,1280]{1,0:T(8,128)(2,1)}, bf16[128,1280]{1,0:T(8,128)(2,1)S(1)}, u32[]{:S(2)}, u32[]{:S(2)}) collective-permute-start(bf16[128,1280]{1,0:T(8,128)(2,1)} %collective-permute-done.4), channel_id=1, source_target_pairs={{0,2},{1,3},{4,6},{5,7},{8,10},{9,11},{12,14},{13,15},{16,18},{17,... | collective-permute-start | bytes 983048 | tf_op jit(solution)/shard_map/ppermute | solution.py:235
  22.0 3.7 %copy-start.41 = (f32[1280]{0:T(1024)S(1)}, f32[1280]{0:T(1024)}, u32[]{:S(2)}) copy-start(f32[1280]{0:T(1024)} %get-tuple-element.133) | copy-start | bytes 15364
  22.0 3.7 %copy-start.42 = (f32[1280]{0:T(1024)S(1)}, f32[1280]{0:T(1024)}, u32[]{:S(2)}) copy-start(f32[1280]{0:T(1024)} %get-tuple-element.178) | copy-start | bytes 15364
  23.1 2.6 %copy-start.2 = (bf16[256,1280]{1,0:T(8,128)(2,1)}, bf16[256,1280]{1,0:T(8,128)(2,1)S(1)}, u32[]{:S(2)}) copy-start(bf16[256,1280]{1,0:T(8,128)(2,1)S(1)} %select_dynamic-update-slice_fusion.1) | copy-start | bytes 1966084
  23.1 7.5 %slice-start = ((s8[5242880]{0:T(1024)(128)(4,1)}), s8[4194304]{0:T(1024)(128)(4,1)S(1)}, s32[]{:S(2)}) async-start(s8[5242880]{0:T(1024)(128)(4,1)} %bitcast.219), calls=%async_computation | async-start | bytes 8388608
  25.7 4.9 %slice-start.1 = ((s8[5242880]{0:T(1024)(128)(4,1)}), s8[1048576]{0:T(1024)(128)(4,1)S(1)}, s32[]{:S(2)}) async-start(s8[5242880]{0:T(1024)(128)(4,1)} %bitcast.219), calls=%async_computation.1 | async-start | bytes 2097152
  26.3 5.6 %copy-start.7 = (bf16[256,1280]{1,0:T(8,128)(2,1)}, bf16[256,1280]{1,0:T(8,128)(2,1)S(1)}, u32[]{:S(2)}) copy-start(bf16[256,1280]{1,0:T(8,128)(2,1)S(1)} %get-tuple-element.161) | copy-start | bytes 1966084
  26.3 6.9 %copy-start.10 = (bf16[256,1280]{1,0:T(8,128)(2,1)}, bf16[256,1280]{1,0:T(8,128)(2,1)S(1)}, u32[]{:S(2)}) copy-start(bf16[256,1280]{1,0:T(8,128)(2,1)S(1)} %get-tuple-element.162) | copy-start | bytes 1966084
  28.6 5.2 %copy-start.22 = (bf16[256,512]{1,0:T(8,128)(2,1)}, bf16[256,512]{1,0:T(8,128)(2,1)S(1)}, u32[]{:S(2)}) copy-start(bf16[256,512]{1,0:T(8,128)(2,1)S(1)} %fusion.130) | copy-start | bytes 786436
  30.6 3.1 %copy-start.23 = (bf16[256,512]{1,0:T(8,128)(2,1)}, bf16[256,512]{1,0:T(8,128)(2,1)S(1)}, u32[]{:S(2)}) copy-start(bf16[256,512]{1,0:T(8,128)(2,1)S(1)} %fusion.139) | copy-start | bytes 786436
  38.4 2.8 %copy-start.37 = (bf16[256,8,64]{0,2,1:T(8,128)(2,1)}, bf16[256,8,64]{0,2,1:T(8,128)(2,1)S(1)}, u32[]{:S(2)}) copy-start(bf16[256,8,64]{0,2,1:T(8,128)(2,1)S(1)} %convolution_bitcast_fusion) | copy-start | bytes 786436
  38.4 8.0 %copy-start.24 = (bf16[256,512]{1,0:T(8,128)(2,1)S(1)}, bf16[256,512]{1,0:T(8,128)(2,1)}, u32[]{:S(2)}) copy-start(bf16[256,512]{1,0:T(8,128)(2,1)} %fusion.127) | copy-start | bytes 786436
  38.4 8.1 %copy-start.36 = (bf16[256,512]{1,0:T(8,128)(2,1)S(1)}, bf16[256,512]{1,0:T(8,128)(2,1)}, u32[]{:S(2)}) copy-start(bf16[256,512]{1,0:T(8,128)(2,1)} %fusion.145) | copy-start | bytes 786436
  41.2 18.2 %collective-permute-start.7 = (bf16[256,1280]{1,0:T(8,128)(2,1)}, bf16[256,1280]{1,0:T(8,128)(2,1)}, u32[]{:S(2)}, u32[]{:S(2)}) collective-permute-start(bf16[256,1280]{1,0:T(8,128)(2,1)} %convolution_convert_fusion.8), channel_id=1, source_target_pairs={{0,3},{1,2},{4,7},{5,6},{8,11},{9,10},{12,15},{13,14},{16,19},{17,... | collective-permute-start | bytes 1966088 | tf_op jit(solution)/shard_map/ppermute | solution.py:235
  44.2 15.2 %collective-permute-start.6 = (bf16[256,1280]{1,0:T(8,128)(2,1)}, bf16[256,1280]{1,0:T(8,128)(2,1)}, u32[]{:S(2)}, u32[]{:S(2)}) collective-permute-start(bf16[256,1280]{1,0:T(8,128)(2,1)} %convolution_convert_fusion.8), channel_id=1, source_target_pairs={{0,2},{1,3},{4,6},{5,7},{8,10},{9,11},{12,14},{13,15},{16,18},{17,... | collective-permute-start | bytes 1966088 | tf_op jit(solution)/shard_map/ppermute | solution.py:235
  48.8 1.9 copy-start.8
  52.5 4.1 %copy-start.25 = (bf16[256,512]{1,0:T(8,128)(2,1)}, bf16[256,512]{1,0:T(8,128)(2,1)S(1)}, u32[]{:S(2)}) copy-start(bf16[256,512]{1,0:T(8,128)(2,1)S(1)} %fusion.133) | copy-start | bytes 786436
  54.7 2.0 copy-start.38
  56.6 9.5 %copy-start.3 = (bf16[256,1280]{1,0:T(8,128)(2,1)S(1)}, bf16[256,1280]{1,0:T(8,128)(2,1)}, u32[]{:S(2)}) copy-start(bf16[256,1280]{1,0:T(8,128)(2,1)} %copy-done.2) | copy-start | bytes 1966084
  56.6 9.5 %collective-permute-start.3 = (bf16[256,1280]{1,0:T(8,128)(2,1)S(1)}, bf16[256,1280]{1,0:T(8,128)(2,1)S(1)}, u32[]{:S(2)}, u32[]{:S(2)}) collective-permute-start(bf16[256,1280]{1,0:T(8,128)(2,1)S(1)} %convolution_convert_fusion.9), channel_id=1, source_target_pairs={{0,3},{1,2},{4,7},{5,6},{8,11},{9,10},{12,15},{13,14},{16,19},{17,... | collective-permute-start | bytes 1966088 | tf_op jit(solution)/shard_map/ppermute | solution.py:235
  58.1 8.0 %collective-permute-start.2 = (bf16[256,1280]{1,0:T(8,128)(2,1)S(1)}, bf16[256,1280]{1,0:T(8,128)(2,1)S(1)}, u32[]{:S(2)}, u32[]{:S(2)}) collective-permute-start(bf16[256,1280]{1,0:T(8,128)(2,1)S(1)} %convolution_convert_fusion.9), channel_id=1, source_target_pairs={{0,2},{1,3},{4,6},{5,7},{8,10},{9,11},{12,14},{13,15},{16,18},{17,... | collective-permute-start | bytes 1966088 | tf_op jit(solution)/shard_map/ppermute | solution.py:235
  61.9 61.7 %collective-permute-start.11 = (bf16[256,1280]{1,0:T(8,128)(2,1)}, bf16[256,1280]{1,0:T(8,128)(2,1)S(1)}, u32[]{:S(2)}, u32[]{:S(2)}) collective-permute-start(bf16[256,1280]{1,0:T(8,128)(2,1)} %get-tuple-element.143), channel_id=1, source_target_pairs={{2,0},{3,1},{6,4},{7,5},{10,8},{11,9},{14,12},{15,13},{18,16},{19,... | collective-permute-start | bytes 1966088 | tf_op jit(solution)/shard_map/ppermute | solution.py:235
  66.2 10.2 %slice-start.2 = ((s8[5242880]{0:T(1024)(128)(4,1)}), s8[1048576]{0:T(1024)(128)(4,1)S(1)}, s32[]{:S(2)}) async-start(s8[5242880]{0:T(1024)(128)(4,1)} %bitcast.221), calls=%async_computation.2 | async-start | bytes 2097152
  68.7 7.6 %slice-start.3 = ((s8[5242880]{0:T(1024)(128)(4,1)}), s8[4194304]{0:T(1024)(128)(4,1)S(1)}, s32[]{:S(2)}) async-start(s8[5242880]{0:T(1024)(128)(4,1)} %bitcast.221), calls=%async_computation.3 | async-start | bytes 8388608
  70.7 3.1 %copy-start.26 = (bf16[256,1280]{1,0:T(8,128)(2,1)}, bf16[256,1280]{1,0:T(8,128)(2,1)S(1)}, u32[]{:S(2)}) copy-start(bf16[256,1280]{1,0:T(8,128)(2,1)S(1)} %get-tuple-element.159) | copy-start | bytes 1966084
  70.7 6.9 %copy-start.28 = (bf16[256,1280]{1,0:T(8,128)(2,1)}, bf16[256,1280]{1,0:T(8,128)(2,1)S(1)}, u32[]{:S(2)}) copy-start(bf16[256,1280]{1,0:T(8,128)(2,1)S(1)} %get-tuple-element.160) | copy-start | bytes 1966084
  77.6 4.8 %copy-start.32 = (bf16[64,512]{0,1:T(8,128)(2,1)S(1)}, bf16[64,512]{0,1:T(8,128)(2,1)}, u32[]{:S(2)}) copy-start(bf16[64,512]{0,1:T(8,128)(2,1)} %copy.113) | copy-start | bytes 196612
  77.6 4.8 %copy-start.44 = (pred[64,256]{1,0:T(8,128)(4,1)S(1)}, pred[64,256]{1,0:T(8,128)(4,1)}, u32[]{:S(2)}) copy-start(pred[64,256]{1,0:T(8,128)(4,1)} %broadcast_compare_fusion.2) | copy-start | bytes 49156
  84.5 2.3 copy-start.13
  84.5 3.2 %copy-start.16 = (bf16[64,512]{0,1:T(8,128)(2,1)S(1)}, bf16[64,512]{0,1:T(8,128)(2,1)}, u32[]{:S(2)}) copy-start(bf16[64,512]{0,1:T(8,128)(2,1)} %copy.114) | copy-start | bytes 196612
  86.9 6.7 %copy-start.45 = (pred[64,256]{1,0:T(8,128)(4,1)S(1)}, pred[64,256]{1,0:T(8,128)(4,1)}, u32[]{:S(2)}) copy-start(pred[64,256]{1,0:T(8,128)(4,1)} %broadcast_compare_fusion.3) | copy-start | bytes 49156
  88.7 34.8 %collective-permute-start.8 = (bf16[256,1280]{1,0:T(8,128)(2,1)}, bf16[256,1280]{1,0:T(8,128)(2,1)}, u32[]{:S(2)}, u32[]{:S(2)}) collective-permute-start(bf16[256,1280]{1,0:T(8,128)(2,1)} %get-tuple-element.141), channel_id=1, source_target_pairs={{2,0},{3,1},{6,4},{7,5},{10,8},{11,9},{14,12},{15,13},{18,16},{19,... | collective-permute-start | bytes 1966088 | tf_op jit(solution)/shard_map/ppermute | solution.py:235
  95.8 1.9 copy-start.34
  95.8 9.0 %slice-start.4 = ((s8[5242880]{0:T(1024)(128)(4,1)}), s8[4194304]{0:T(1024)(128)(4,1)S(1)}, s32[]{:S(2)}) async-start(s8[5242880]{0:T(1024)(128)(4,1)} %bitcast.223), calls=%async_computation.4 | async-start | bytes 8388608
  97.9 6.8 %slice-start.5 = ((s8[5242880]{0:T(1024)(128)(4,1)}), s8[1048576]{0:T(1024)(128)(4,1)S(1)}, s32[]{:S(2)}) async-start(s8[5242880]{0:T(1024)(128)(4,1)} %bitcast.223), calls=%async_computation.5 | async-start | bytes 2097152
  99.9 4.5 %copy-start.14 = (f32[8,64,256]{2,1,0:T(8,128)S(1)}, f32[8,64,256]{2,1,0:T(8,128)}, u32[]{:S(2)}) copy-start(f32[8,64,256]{2,1,0:T(8,128)} %get-tuple-element.173) | copy-start | bytes 1572868
  99.9 4.5 %copy-start.33 = (bf16[64,512]{0,1:T(8,128)(2,1)S(1)}, bf16[64,512]{0,1:T(8,128)(2,1)}, u32[]{:S(2)}) copy-start(bf16[64,512]{0,1:T(8,128)(2,1)} %copy.113) | copy-start | bytes 196612
  101.8 12.3 %collective-permute-start.10 = (bf16[256,1280]{1,0:T(8,128)(2,1)S(1)}, bf16[256,1280]{1,0:T(8,128)(2,1)S(1)}, u32[]{:S(2)}, u32[]{:S(2)}) collective-permute-start(bf16[256,1280]{1,0:T(8,128)(2,1)S(1)} %fusion.59), channel_id=1, source_target_pairs={{2,1},{3,0},{6,5},{7,4},{10,9},{11,8},{14,13},{15,12},{18,17},{19,... | collective-permute-start | bytes 1966088 | tf_op jit(solution)/shard_map/ppermute | solution.py:235
  103.1 15.5 %collective-permute-start.9 = (bf16[256,1280]{1,0:T(8,128)(2,1)S(1)}, bf16[256,1280]{1,0:T(8,128)(2,1)S(1)}, u32[]{:S(2)}, u32[]{:S(2)}) collective-permute-start(bf16[256,1280]{1,0:T(8,128)(2,1)S(1)} %fusion.59), channel_id=1, source_target_pairs={{2,0},{3,1},{6,4},{7,5},{10,8},{11,9},{14,12},{15,13},{18,16},{19,... | collective-permute-start | bytes 1966088 | tf_op jit(solution)/shard_map/ppermute | solution.py:235
  105.7 1.1 copy-start.27
  105.7 1.3 copy-start.29
  107.8 2.3 copy-start.12
  107.8 2.5 %copy-start.35 = (bf16[8,64,64]{2,1,0:T(8,128)(2,1)S(1)}, bf16[8,64,64]{2,1,0:T(8,128)(2,1)}, u32[]{:S(2)}) copy-start(bf16[8,64,64]{2,1,0:T(8,128)(2,1)} %convolution_convert_fusion.12) | copy-start | bytes 196612
  107.8 13.3 %collective-permute-start.13 = (bf16[256,1280]{1,0:T(8,128)(2,1)S(1)}, bf16[256,1280]{1,0:T(8,128)(2,1)S(1)}, u32[]{:S(2)}, u32[]{:S(2)}) collective-permute-start(bf16[256,1280]{1,0:T(8,128)(2,1)S(1)} %fusion.60), channel_id=1, source_target_pairs={{2,1},{3,0},{6,5},{7,4},{10,9},{11,8},{14,13},{15,12},{18,17},{19,... | collective-permute-start | bytes 1966088 | tf_op jit(solution)/shard_map/ppermute | solution.py:235
  114.1 8.2 %collective-permute-start.12 = (bf16[256,1280]{1,0:T(8,128)(2,1)S(1)}, bf16[256,1280]{1,0:T(8,128)(2,1)S(1)}, u32[]{:S(2)}, u32[]{:S(2)}) collective-permute-start(bf16[256,1280]{1,0:T(8,128)(2,1)S(1)} %fusion.60), channel_id=1, source_target_pairs={{2,0},{3,1},{6,4},{7,5},{10,8},{11,9},{14,12},{15,13},{18,16},{19,... | collective-permute-start | bytes 1966088 | tf_op jit(solution)/shard_map/ppermute | solution.py:235
  123.5 4.0 %copy-start.4 = (f32[256,1280]{1,0:T(8,128)S(1)}, f32[256,1280]{1,0:T(8,128)}, u32[]{:S(2)}) copy-start(f32[256,1280]{1,0:T(8,128)} %get-tuple-element.55) | copy-start | bytes 3932164 | tf_op jit(solution)/shard_map/cond
  123.5 4.0 %copy-start.5 = (f32[256,1280]{1,0:T(8,128)S(1)}, f32[256,1280]{1,0:T(8,128)}, u32[]{:S(2)}) copy-start(f32[256,1280]{1,0:T(8,128)} %get-tuple-element.54) | copy-start | bytes 3932164 | tf_op jit(solution)/shard_map/cond
  134.0 2.1 copy-start.30
  145.2 7.3 %copy-start.9 = (bf16[256,1280]{1,0:T(8,128)(2,1)S(1)}, bf16[256,1280]{1,0:T(8,128)(2,1)}, u32[]{:S(2)}) copy-start(bf16[256,1280]{1,0:T(8,128)(2,1)} %get-tuple-element.66) | copy-start | bytes 1966084 | tf_op jit(solution)/shard_map/cond
  152.5 1.2 copy-start.39
  152.5 1.2 copy-start.40
  158.0 1.3 copy-start.15
  238.5 3.9 %copy-start.1 = (bf16[2,64,1280]{2,1,0:T(8,128)(2,1)S(1)}, bf16[2,64,1280]{2,1,0:T(8,128)(2,1)}, u32[]{:S(2)}) copy-start(bf16[2,64,1280]{2,1,0:T(8,128)(2,1)} %param.12) | copy-start | bytes 983044
  (6 other events, 5.6 us)

commit v2 on v1

v2 whole, which is shorter than its diff:
```python
import functools
import math

import jax
import jax.numpy as jnp
from jax import lax
from jax.experimental import pallas as pl
from jax.experimental.pallas import tpu as pltpu
from jax.sharding import PartitionSpec as P

HS = 64
EPSILON = 1e-05
MESH = pl.DeviceIdType.MESH
F32 = jnp.float32
BF16 = jnp.bfloat16
NEAR = 2
CHUNKS = 4


def dot_rows(left, right):
    return lax.dot_general(left, right, (((1,), (1,)), ((), ())), preferred_element_type=F32)


def dot_plain(left, right):
    return lax.dot_general(left, right, (((1,), (0,)), ((), ())), preferred_element_type=F32)


def dot_outer(left, right):
    return lax.dot_general(left, right, (((0,), (0,)), ((), ())), preferred_element_type=F32)


def standardize(values):
    center = values - jnp.mean(values, axis=-1, keepdims=True)
    inverse = lax.rsqrt(jnp.mean(center * center, axis=-1, keepdims=True) + EPSILON)
    return center * inverse, inverse


def flat(rows):
    return rows.reshape(rows.shape[0] * rows.shape[1], rows.shape[2])


def utterance_ids(lengths_ref, m, shape, dim):
    places = lax.broadcasted_iota(jnp.int32, shape, dim)
    ids = jnp.zeros(shape, jnp.int32)
    bound = jnp.int32(0)
    for utterance in range(lengths_ref.shape[1]):
        bound = bound + lengths_ref[m, utterance]
        ids = ids + jnp.where(places >= bound, 1, 0)
    return ids


def mask_bias(frame_lens, other_lens, m, frame_count, other_count):
    shape = (frame_count, other_count)
    same = utterance_ids(frame_lens, m, shape, 0) == utterance_ids(other_lens, m, shape, 1)
    return jnp.where(same, 0.0, -1e30).astype(F32)


def head_probs(key_rows, queries, bias):
    scores = dot_rows(key_rows, queries) + bias
    raised = jnp.exp(scores - jnp.max(scores, axis=0, keepdims=True))
    return raised * (1.0 / jnp.sum(raised, axis=0, keepdims=True))


def head_scores_grad(probs, value_rows, grad_rows):
    grad_probs = dot_rows(value_rows, grad_rows)
    return (probs * (grad_probs - jnp.sum(grad_probs * probs, axis=0, keepdims=True))).astype(BF16)


def section_kernel(
    parts, frame_lens, token_lens, frames, tokens, upstream, weights, gains, biases, terms,
    full, normed, queries, key_rows, value_rows, context, probs, part, inbox, states, state_grad,
    key_grad, value_grad, bias, dec_bias, dec_queries, dec_grad, dec_context,
    frame_send, frame_recv, pass_send, pass_recv, part_send, part_recv, state_send, state_recv,
):
    section = lax.axis_index("segment")
    place = lax.axis_index("mp")
    micro_count, shard_rows, features = frames.shape
    frame_count = shard_rows * parts
    token_count = tokens.shape[1]
    head_cols = weights.shape[1]
    heads = head_cols // HS
    scaling = 1.0 / math.sqrt(HS)

    barrier = pltpu.get_barrier_semaphore()
    for apart in range(parts):
        for side in range(2):
            if apart == 0 and side == 0:
                continue
            pl.semaphore_signal(
                barrier,
                inc=1,
                device_id={
                    "segment": lax.rem(section + side, 2),
                    "mp": lax.rem(place + apart, parts),
                },
                device_id_type=MESH,
            )
    pl.semaphore_wait(barrier, 2 * parts - 1)

    def copy_to(source, target, sends, recvs, side, apart):
        return pltpu.make_async_remote_copy(
            src_ref=source,
            dst_ref=target,
            send_sem=sends,
            recv_sem=recvs,
            device_id={"segment": side, "mp": lax.rem(place + apart, parts)},
            device_id_type=MESH,
        )

    def frame_copy(m, apart):
        return copy_to(
            frames.at[m], full.at[m, place], frame_send.at[m, apart], frame_recv.at[m, apart],
            0, apart,
        )

    def pass_copy(m, apart):
        origin = lax.rem(place - apart + parts, parts)
        return copy_to(
            full.at[m, origin], full.at[m, origin], pass_send.at[m, apart],
            pass_recv.at[m, apart], 1, 0,
        )

    def part_copy(m, apart, side):
        return copy_to(
            part.at[m], inbox.at[m, apart], part_send.at[m, apart], part_recv.at[m, apart],
            side, apart,
        )

    def state_copy(m):
        return copy_to(states.at[m], states.at[m], state_send.at[m], state_recv.at[m], 0, 0)

    def send_parts(m, side):
        for apart in range(1, parts):
            part_copy(m, apart, side).start()
        part_copy(m, 0, side).start()

    def received_sum(m, side):
        total = None
        for apart in range(parts):
            part_copy(m, apart, side).wait_recv()
            piece = inbox[m, apart].astype(F32)
            total = piece if total is None else total + piece
        return total

    def store_terms(last_left, last_right):
        block = min(256, head_cols)
        sources = ((key_grad, normed), (value_grad, normed), (last_left, last_right))
        for index, (left, right) in enumerate(sources):
            wide = flat(right[...])
            for start in range(0, head_cols, block):
                columns = slice(start, start + block)
                terms[index, columns, :] = dot_outer(flat(left[:, :, columns]), wide).astype(BF16)

    def encoder_forward(m, carry):
        for apart in range(1, parts):
            frame_copy(m, apart).wait_recv()
        for apart in range(1, parts):
            pass_copy(m, apart).start()
        rows, _ = standardize(flat(full[m]).astype(F32))
        normed[m] = (rows * gains[0:1, :] + biases[0:1, :]).astype(BF16)
        row_input = normed[m]
        queries[m] = (dot_rows(row_input, weights[0]).astype(BF16) * scaling).astype(BF16)
        key_rows[m] = dot_rows(row_input, weights[1]).astype(BF16)
        value_rows[m] = dot_rows(row_input, weights[2]).astype(BF16)
        bias[...] = mask_bias(frame_lens, frame_lens, m, frame_count, frame_count)
        for h in range(heads):
            cols = slice(h * HS, (h + 1) * HS)
            head = head_probs(key_rows[m, :, cols], queries[m, :, cols], bias[...]).astype(BF16)
            probs[m, h] = head
            context[m, :, cols] = dot_outer(head, value_rows[m, :, cols]).astype(BF16)
        part[m] = dot_plain(context[m], weights[3]).astype(BF16)
        send_parts(m, 1)
        return carry

    def encoder_backward(m, carry):
        grad_out = received_sum(m, 0)
        state_copy(m).wait_recv()
        rows, inverse = standardize(states[m].astype(F32))
        scaled = grad_out * gains[2:3, :]
        state_grad[m] = (
            inverse
            * (
                scaled
                - jnp.mean(scaled, axis=-1, keepdims=True)
                - rows * jnp.mean(scaled * rows, axis=-1, keepdims=True)
            )
        ).astype(BF16)
        grad_rows = dot_rows(state_grad[m], weights[3]).astype(BF16)
        key_rows[m] = grad_rows
        for h in range(heads):
            cols = slice(h * HS, (h + 1) * HS)
            grad_head = key_rows[m, :, cols]
            head = probs[m, h]
            change = head_scores_grad(head.astype(F32), value_rows[m, :, cols], grad_head)
            key_grad[m, :, cols] = dot_plain(change, queries[m, :, cols]).astype(BF16)
            value_grad[m, :, cols] = dot_plain(head, grad_head).astype(BF16)
        return carry

    def decoder_step(m, carry):
        for apart in range(1, parts):
            pass_copy(m, apart).wait_recv()
        total = received_sum(m, 1)
        states[m] = (flat(full[m]).astype(F32) + total).astype(BF16)
        state_copy(m).start()
        rows, _ = standardize(states[m].astype(F32))
        normed[m] = (rows * gains[2:3, :] + biases[2:3, :]).astype(BF16)
        row_input = normed[m]
        key_rows[m] = dot_rows(row_input, weights[1]).astype(BF16)
        value_rows[m] = dot_rows(row_input, weights[2]).astype(BF16)
        dec_bias[...] = mask_bias(frame_lens, token_lens, m, frame_count, token_count)
        for h in range(heads):
            cols = slice(h * HS, (h + 1) * HS)
            query_head = dec_queries[m, :, cols]
            value_head = value_rows[m, :, cols]
            grad_head = dec_grad[m, :, cols]
            exact = head_probs(key_rows[m, :, cols], query_head, dec_bias[...])
            head = exact.astype(BF16)
            dec_context[m, :, cols] = dot_outer(head, value_head).astype(BF16)
            change = head_scores_grad(exact, value_head, grad_head)
            key_grad[m, :, cols] = dot_plain(change, query_head).astype(BF16)
            value_grad[m, :, cols] = dot_plain(head, grad_head).astype(BF16)
        part[m] = (
            dot_plain(key_grad[m], weights[1]) + dot_plain(value_grad[m], weights[2])
        ).astype(BF16)
        send_parts(m, 0)
        return carry

    @pl.when(section == 0)
    def _():
        for m in range(micro_count):
            for apart in range(1, parts):
                frame_copy(m, apart).start()
        for m in range(micro_count):
            full[m, place] = frames[m]
        lax.fori_loop(0, micro_count, encoder_forward, 0)
        lax.fori_loop(0, micro_count, encoder_backward, 0)
        store_terms(context, state_grad)
        for m in range(micro_count):
            for apart in range(1, parts):
                frame_copy(m, apart).wait_send()
                pass_copy(m, apart).wait_send()
            for apart in range(parts):
                part_copy(m, apart, 1).wait_send()

    @pl.when(section == 1)
    def _():
        for m in range(micro_count):
            full[m, place] = frames[m]
        rows, _ = standardize(flat(tokens[...]).astype(F32))
        token_rows = (rows * gains[1:2, :] + biases[1:2, :]).astype(BF16)
        small = (micro_count, token_count, head_cols)
        token_queries = dot_rows(token_rows, weights[0]).astype(BF16) * scaling
        dec_queries[...] = token_queries.astype(BF16).reshape(small)
        dec_grad[...] = dot_rows(flat(upstream[...]), weights[3]).astype(BF16).reshape(small)
        lax.fori_loop(0, micro_count, decoder_step, 0)
        store_terms(dec_context, upstream)
        for m in range(micro_count):
            state_copy(m).wait_send()
            for apart in range(parts):
                part_copy(m, apart, 0).wait_send()


def section_terms(
    frames, dec_states, out_grad, frame_lengths, token_lengths, matrices, norm_gains, norm_biases
):
    parts = lax.axis_size("mp")
    micro_count, shard_rows, features = frames.shape
    frame_count = shard_rows * parts
    token_count = dec_states.shape[1]
    head_cols = matrices.shape[1]
    dma = pltpu.SemaphoreType.DMA
    wide = pltpu.VMEM((micro_count, frame_count, features), BF16)
    thin = pltpu.VMEM((micro_count, frame_count, head_cols), BF16)
    small = pltpu.VMEM((micro_count, token_count, head_cols), BF16)
    pairs = dma((micro_count, parts))
    return pl.pallas_call(
        functools.partial(section_kernel, parts),
        out_shape=jax.ShapeDtypeStruct((3, head_cols, features), BF16),
        in_specs=[pl.BlockSpec(memory_space=pltpu.SMEM)] * 2
        + [pl.BlockSpec(memory_space=pltpu.VMEM)] * 6,
        out_specs=pl.BlockSpec(memory_space=pltpu.VMEM),
        scratch_shapes=[
            pltpu.VMEM((micro_count, parts, shard_rows, features), BF16),
            wide,
            thin,
            thin,
            thin,
            thin,
            pltpu.VMEM((micro_count, head_cols // HS, frame_count, frame_count), BF16),
            wide,
            pltpu.VMEM((micro_count, parts, frame_count, features), BF16),
            wide,
            wide,
            thin,
            thin,
            pltpu.VMEM((frame_count, frame_count), F32),
            pltpu.VMEM((frame_count, token_count), F32),
            small,
            small,
            small,
            pairs,
            pairs,
            pairs,
            pairs,
            pairs,
            pairs,
            dma((micro_count,)),
            dma((micro_count,)),
        ],
        compiler_params=pltpu.CompilerParams(
            collective_id=1, has_side_effects=True, vmem_limit_bytes=52 * 1024 * 1024
        ),
    )(
        frame_lengths[:, 0], token_lengths[:, 0], frames, dec_states, out_grad, matrices,
        norm_gains, norm_biases,
    )


def sum_kernel(
    near, far, chunks, g_ref, out_ref, near_in, held, far_in,
    near_send, near_recv, far_send, far_recv, back_send, back_recv, last_send, last_recv,
):
    me = lax.axis_index("dp")
    b = lax.rem(me, near)
    a = lax.div(me, near)
    other = a * near + (1 - b)

    def far_peer(apart):
        return lax.rem(a + apart, far) * near + b

    barrier = pltpu.get_barrier_semaphore()
    pl.semaphore_signal(barrier, inc=1, device_id={"dp": other}, device_id_type=MESH)
    for apart in range(1, far):
        pl.semaphore_signal(barrier, inc=1, device_id={"dp": far_peer(apart)}, device_id_type=MESH)
    pl.semaphore_wait(barrier, far)

    def near_copy(k):
        return pltpu.make_async_remote_copy(
            src_ref=g_ref.at[k, 1 - b],
            dst_ref=near_in.at[k],
            send_sem=near_send.at[k],
            recv_sem=near_recv.at[k],
            device_id={"dp": other},
            device_id_type=MESH,
        )

    def far_copy(k, apart):
        return pltpu.make_async_remote_copy(
            src_ref=held.at[k, lax.rem(a + apart, far)],
            dst_ref=far_in.at[k, apart - 1],
            send_sem=far_send.at[k, apart - 1],
            recv_sem=far_recv.at[k, apart - 1],
            device_id={"dp": far_peer(apart)},
            device_id_type=MESH,
        )

    def back_copy(k, apart):
        return pltpu.make_async_remote_copy(
            src_ref=out_ref.at[k, b, a],
            dst_ref=out_ref.at[k, b, a],
            send_sem=back_send.at[k, apart - 1],
            recv_sem=back_recv.at[k, apart - 1],
            device_id={"dp": far_peer(apart)},
            device_id_type=MESH,
        )

    def last_copy(k):
        return pltpu.make_async_remote_copy(
            src_ref=out_ref.at[k, b],
            dst_ref=out_ref.at[k, b],
            send_sem=last_send.at[k],
            recv_sem=last_recv.at[k],
            device_id={"dp": other},
            device_id_type=MESH,
        )

    def step_far(k):
        near_copy(k).wait_recv()
        if k + 2 < chunks:
            near_copy(k + 2).start()
        held[k] = (g_ref[k, b].astype(F32) + near_in[k].astype(F32)).astype(BF16)
        for apart in range(1, far):
            far_copy(k, apart).start()

    def step_back(k):
        total = held[k, a].astype(F32)
        for apart in range(1, far):
            far_copy(k, apart).wait_recv()
            total = total + far_in[k, apart - 1].astype(F32)
        out_ref[k, b, a] = total.astype(BF16)
        for apart in range(1, far):
            back_copy(k, apart).start()

    def step_last(k):
        for apart in range(1, far):
            back_copy(k, apart).wait_recv()
        last_copy(k).start()

    for k in range(min(2, chunks)):
        near_copy(k).start()
    for tick in range(chunks + 2):
        if tick < chunks:
            step_far(tick)
        if 0 <= tick - 1 < chunks:
            step_back(tick - 1)
        if 0 <= tick - 2 < chunks:
            step_last(tick - 2)
    for k in range(chunks):
        last_copy(k).wait_recv()
        near_copy(k).wait_send()
        last_copy(k).wait_send()
        for apart in range(1, far):
            far_copy(k, apart).wait_send()
            back_copy(k, apart).wait_send()


def sum_over_groups(terms):
    near = NEAR
    far = lax.axis_size("dp") // near
    rows, features = terms.shape
    unit = CHUNKS * near * far * 16
    padded = -(-rows // unit) * unit
    if padded != rows:
        terms = jnp.pad(terms, ((0, padded - rows), (0, 0)))
    piece = padded // (CHUNKS * near * far)
    blocks = terms.reshape(CHUNKS, near, far, piece, features)
    dma = pltpu.SemaphoreType.DMA
    out = pl.pallas_call(
        functools.partial(sum_kernel, near, far, CHUNKS),
        out_shape=jax.ShapeDtypeStruct(blocks.shape, BF16),
        in_specs=[pl.BlockSpec(memory_space=pltpu.VMEM)],
        out_specs=pl.BlockSpec(memory_space=pltpu.VMEM),
        scratch_shapes=[
            pltpu.VMEM((CHUNKS, far, piece, features), BF16),
            pltpu.VMEM((CHUNKS, far, piece, features), BF16),
            pltpu.VMEM((CHUNKS, far - 1, piece, features), BF16),
            dma((CHUNKS,)),
            dma((CHUNKS,)),
            dma((CHUNKS, far - 1)),
            dma((CHUNKS, far - 1)),
            dma((CHUNKS, far - 1)),
            dma((CHUNKS, far - 1)),
            dma((CHUNKS,)),
            dma((CHUNKS,)),
        ],
        compiler_params=pltpu.CompilerParams(
            collective_id=0, has_side_effects=True, vmem_limit_bytes=40 * 1024 * 1024
        ),
    )(blocks)
    return out.reshape(padded, features)[:rows]


def shards(
    frames, dec_states, out_grad, frame_lengths, token_lengths, weights, norm_gains, norm_biases
):
    matrices = weights[0]
    head_cols, features = matrices.shape[1:]
    terms = section_terms(
        frames, dec_states, out_grad, frame_lengths, token_lengths, matrices, norm_gains,
        norm_biases,
    )
    gradient = sum_over_groups(terms.reshape(3 * head_cols, features)).astype(F32)
    return gradient.reshape(1, 3, head_cols, features)


def solution(mesh):
    placed = (
        P(None, ("dp", "mp"), None),
        P(None, "dp", None),
        P(None, "dp", None),
        P(None, "dp", None),
        P(None, "dp", None),
        P("segment", None, "mp", None),
        P(),
        P(),
    )
    return jax.shard_map(
        shards,
        mesh=mesh,
        in_specs=placed,
        out_specs=P("segment", None, "mp", None),
        check_vma=False,
    )
```

time: 244 us -> 171 us (0.70)
  the two profiles are of different devices: /device:TPU:0 before, /device:TPU:26 now
where the time goes in v2:
time: 171 us; the launch traced here: 170 us
  Pallas kernels  159 us (93%)
  local copies, waits for them, and re-layouts  7.95 us (5%)
  other arithmetic  3.88 us (2%)
    pallas_call x1, Pallas kernels, sum_over_groups(): pl.pallas_call(functools.partial(sum_kernel, near, far, CHUNKS), out_shap...  106 us
    pallas_call x1, Pallas kernels, section_terms(): pl.pallas_call(functools.partial(section_kernel, parts), out_shape=jax.Sh...  52.2 us
    unnamed x16, local copies, waits for them, and re-layouts  7.95 us
    convert_element_type x1, other arithmetic, shards(): sum_over_groups(terms.reshape(3 * head_cols, features)).astype(F32)  3.88 us

profile of v2, /device:TPU:26, one launch (start us, length us, event | category | flops | bytes accessed | tf_op | source)
XLA Modules:
  0.0 170.5 jit_solution(5110675337562543076)
XLA Ops:
  0.0 0.0 copy-start.1
  0.0 1.1 copy-done.1
  1.1 0.0 copy-start.2
  1.1 1.0 copy-done.2
  2.1 0.0 copy-start.3
  2.1 1.0 copy-done.3
  3.0 0.0 copy-start.4
  3.0 0.7 copy-done.4
  3.8 0.0 copy-start.5
  3.8 0.7 copy-done.5
  4.5 0.0 copy-start.6
  4.5 0.7 copy-done.6
  5.2 0.0 copy-start.7
  5.2 0.7 copy-done.7
  5.8 52.2 %shard_map.82 = bf16[3,512,1280]{2,1,0:T(8,128)(2,1)} custom-call(s32[2,4]{1,0:T(2,128)S(1)} %bitcast.8, s32[2,4]{1,0:T(2,128)S(1)} %bitcast.9, bf16[2,128,1280]{2,1,0:T(8,128)(2,1)S(1)} %copy-done.1, bf16[2,64,1280]{2,1,0:T(8,128)(2,1)S(1)} %copy-done.2, bf16[2,64,1280]{2,1,0:T(8,128)(2,1)S(1)} %copy-done.3, bf16[4,512,1280]{2,1,0:T(8,128)(2,1)} %bitcast.10, ...), custom_call_target="tpu_custom_call" | custom-call | tf_op jit(solution)/shard_map/pallas_call | solution.py:276
  58.0 0.0 copy-start
  58.0 2.1 %copy-done = bf16[3,512,1280]{2,1,0:T(8,128)(2,1)S(1)} copy-done((bf16[3,512,1280]{2,1,0:T(8,128)(2,1)S(1)}, bf16[3,512,1280]{2,1,0:T(8,128)(2,1)}, u32[]{:S(2)}) %copy-start) | copy-done | bytes 3932184
  60.1 106.4 %shard_map.83 = bf16[4,2,4,48,1280]{4,3,2,1,0:T(8,128)(2,1)S(1)} custom-call(bf16[4,2,4,48,1280]{4,3,2,1,0:T(8,128)(2,1)S(1)} %bitcast.7), custom_call_target="tpu_custom_call" | custom-call | tf_op jit(solution)/shard_map/pallas_call | solution.py:428
  166.6 3.9 %convert.1 = f32[1,3,512,1280]{3,2,1,0:T(8,128)} convert(bf16[1,3,512,1280]{3,2,1,0:T(8,128)(2,1)S(1)} %bitcast.6) | non-fusion elementwise | flops 1966080 | bytes 11796480 | tf_op jit(solution)/shard_map/convert_element_type | solution.py:462
Async XLA Ops:
  0.0 1.1 copy-start.1
  1.1 1.0 copy-start.2
  2.1 1.0 copy-start.3
  3.0 0.7 copy-start.4
  3.8 0.7 copy-start.5
  4.5 0.7 copy-start.6
  5.2 0.7 copy-start.7
  58.0 2.1 %copy-start = (bf16[3,512,1280]{2,1,0:T(8,128)(2,1)S(1)}, bf16[3,512,1280]{2,1,0:T(8,128)(2,1)}, u32[]{:S(2)}) copy-start(bf16[3,512,1280]{2,1,0:T(8,128)(2,1)} %shard_map.82) | copy-start | bytes 11796484

commit v3 on v2

--- a/solution.py
+++ b/solution.py
@@ -14,7 +14,7 @@
 F32 = jnp.float32
 BF16 = jnp.bfloat16
 NEAR = 2
-CHUNKS = 4
+CUTS = 2
 
 
 def dot_rows(left, right):
@@ -317,132 +317,121 @@
 
 
 def sum_kernel(
-    near, far, chunks, g_ref, out_ref, near_in, held, far_in,
-    near_send, near_recv, far_send, far_recv, back_send, back_recv, last_send, last_recv,
+    size, cuts, g_ref, out_ref, held, inbox, add_send, add_recv, back_send, back_recv
 ):
+    near = NEAR
+    far = size // near
     me = lax.axis_index("dp")
     b = lax.rem(me, near)
     a = lax.div(me, near)
-    other = a * near + (1 - b)
-
-    def far_peer(apart):
-        return lax.rem(a + apart, far) * near + b
+    place = jnp.where(b == 0, a, 2 * far - 1 - a)
+
+    def device_at(spot):
+        spot = lax.rem(spot + size, size)
+        return jnp.where(spot < far, spot * near, (2 * far - 1 - spot) * near + 1)
+
+    ways = (1, -1)
+    peers = [device_at(place + way) for way in ways]
 
     barrier = pltpu.get_barrier_semaphore()
-    pl.semaphore_signal(barrier, inc=1, device_id={"dp": other}, device_id_type=MESH)
-    for apart in range(1, far):
-        pl.semaphore_signal(barrier, inc=1, device_id={"dp": far_peer(apart)}, device_id_type=MESH)
-    pl.semaphore_wait(barrier, far)
-
-    def near_copy(k):
+    for peer in peers:
+        pl.semaphore_signal(barrier, inc=1, device_id={"dp": peer}, device_id_type=MESH)
+    pl.semaphore_wait(barrier, 2)
+
+    def block(d, apart):
+        return lax.rem(place + ways[d] * apart + 2 * size, size)
+
+    def add_copy(d, c, step, first):
+        source = g_ref.at[d, c, block(d, 0)] if first else held.at[d, c, step - 1]
         return pltpu.make_async_remote_copy(
-            src_ref=g_ref.at[k, 1 - b],
-            dst_ref=near_in.at[k],
-            send_sem=near_send.at[k],
-            recv_sem=near_recv.at[k],
-            device_id={"dp": other},
+            src_ref=source,
+            dst_ref=inbox.at[d, c, step],
+            send_sem=add_send.at[d, c, step],
+            recv_sem=add_recv.at[d, c, step],
+            device_id={"dp": peers[d]},
             device_id_type=MESH,
         )
 
-    def far_copy(k, apart):
+    def back_copy(d, c, step):
+        ref = out_ref.at[d, c, block(d, 1 - step)]
         return pltpu.make_async_remote_copy(
-            src_ref=held.at[k, lax.rem(a + apart, far)],
-            dst_ref=far_in.at[k, apart - 1],
-            send_sem=far_send.at[k, apart - 1],
-            recv_sem=far_recv.at[k, apart - 1],
-            device_id={"dp": far_peer(apart)},
+            src_ref=ref,
+            dst_ref=ref,
+            send_sem=back_send.at[d, c, step],
+            recv_sem=back_recv.at[d, c, step],
+            device_id={"dp": peers[d]},
             device_id_type=MESH,
         )
 
-    def back_copy(k, apart):
-        return pltpu.make_async_remote_copy(
-            src_ref=out_ref.at[k, b, a],
-            dst_ref=out_ref.at[k, b, a],
-            send_sem=back_send.at[k, apart - 1],
-            recv_sem=back_recv.at[k, apart - 1],
-            device_id={"dp": far_peer(apart)},
+    streams = [(d, c) for c in range(cuts) for d in range(2)]
+    last = size - 2
+
+    def summed(d, c, step):
+        mine = g_ref[d, c, block(d, -step - 1)].astype(F32)
+        return (mine + inbox[d, c, step].astype(F32)).astype(BF16)
+
+    for d, c in streams:
+        add_copy(d, c, 0, True).start()
+
+    def add_step(step, carry):
+        for d, c in streams:
+            wait_add(d, c, step)
+            held[d, c, step] = summed(d, c, step)
+            add_copy(d, c, step + 1, False).start()
+        return carry
+
+    def wait_add(d, c, step):
+        pltpu.make_async_remote_copy(
+            src_ref=held.at[d, c, step],
+            dst_ref=inbox.at[d, c, step],
+            send_sem=add_send.at[d, c, step],
+            recv_sem=add_recv.at[d, c, step],
+            device_id={"dp": peers[d]},
             device_id_type=MESH,
-        )
-
-    def last_copy(k):
-        return pltpu.make_async_remote_copy(
-            src_ref=out_ref.at[k, b],
-            dst_ref=out_ref.at[k, b],
-            send_sem=last_send.at[k],
-            recv_sem=last_recv.at[k],
-            device_id={"dp": other},
-            device_id_type=MESH,
-        )
-
-    def step_far(k):
-        near_copy(k).wait_recv()
-        if k + 2 < chunks:
-            near_copy(k + 2).start()
-        held[k] = (g_ref[k, b].astype(F32) + near_in[k].astype(F32)).astype(BF16)
-        for apart in range(1, far):
-            far_copy(k, apart).start()
-
-    def step_back(k):
-        total = held[k, a].astype(F32)
-        for apart in range(1, far):
-            far_copy(k, apart).wait_recv()
-            total = total + far_in[k, apart - 1].astype(F32)
-        out_ref[k, b, a] = total.astype(BF16)
-        for apart in range(1, far):
-            back_copy(k, apart).start()
-
-    def step_last(k):
-        for apart in range(1, far):
-            back_copy(k, apart).wait_recv()
-        last_copy(k).start()
-
-    for k in range(min(2, chunks)):
-        near_copy(k).start()
-    for tick in range(chunks + 2):
-        if tick < chunks:
-            step_far(tick)
-        if 0 <= tick - 1 < chunks:
-            step_back(tick - 1)
-        if 0 <= tick - 2 < chunks:
-            step_last(tick - 2)
-    for k in range(chunks):
-        last_copy(k).wait_recv()
-        near_copy(k).wait_send()
-        last_copy(k).wait_send()
-        for apart in range(1, far):
-            far_copy(k, apart).wait_send()
-            back_copy(k, apart).wait_send()
+        ).wait_recv()
+
+    lax.fori_loop(0, last, add_step, 0)
+    for d, c in streams:
+        wait_add(d, c, last)
+        out_ref[d, c, block(d, 1)] = summed(d, c, last)
+        back_copy(d, c, 0).start()
+
+    def back_step(step, carry):
+        for d, c in streams:
+            back_copy(d, c, step).wait_recv()
+            back_copy(d, c, step + 1).start()
+        return carry
+
+    lax.fori_loop(0, last, back_step, 0)
+    for d, c in streams:
+        back_copy(d, c, last).wait_recv()
+
+    def finish(step, carry):
+        for d, c in streams:
+            add_copy(d, c, step, True).wait_send()
+            back_copy(d, c, step).wait_send()
+        return carry
+
+    lax.fori_loop(0, size - 1, finish, 0)
 
 
 def sum_over_groups(terms):
-    near = NEAR
-    far = lax.axis_size("dp") // near
+    size = lax.axis_size("dp")
     rows, features = terms.shape
-    unit = CHUNKS * near * far * 16
+    unit = 2 * CUTS * size * 16
     padded = -(-rows // unit) * unit
     if padded != rows:
         terms = jnp.pad(terms, ((0, padded - rows), (0, 0)))
-    piece = padded // (CHUNKS * near * far)
-    blocks = terms.reshape(CHUNKS, near, far, piece, features)
-    dma = pltpu.SemaphoreType.DMA
+    piece = padded // (2 * CUTS * size)
+    blocks = terms.reshape(2, CUTS, size, piece, features)
+    slots = pltpu.VMEM((2, CUTS, size - 1, piece, features), BF16)
+    signals = pltpu.SemaphoreType.DMA((2, CUTS, size - 1))
     out = pl.pallas_call(
-        functools.partial(sum_kernel, near, far, CHUNKS),
+        functools.partial(sum_kernel, size, CUTS),
         out_shape=jax.ShapeDtypeStruct(blocks.shape, BF16),
         in_specs=[pl.BlockSpec(memory_space=pltpu.VMEM)],
         out_specs=pl.BlockSpec(memory_space=pltpu.VMEM),
-        scratch_shapes=[
-            pltpu.VMEM((CHUNKS, far, piece, features), BF16),
-            pltpu.VMEM((CHUNKS, far, piece, features), BF16),
-            pltpu.VMEM((CHUNKS, far - 1, piece, features), BF16),
-            dma((CHUNKS,)),
-            dma((CHUNKS,)),
-            dma((CHUNKS, far - 1)),
-            dma((CHUNKS, far - 1)),
-            dma((CHUNKS, far - 1)),
-            dma((CHUNKS, far - 1)),
-            dma((CHUNKS,)),
-            dma((CHUNKS,)),
-        ],
+        scratch_shapes=[slots, slots, signals, signals, signals, signals],
         compiler_params=pltpu.CompilerParams(
             collective_id=0, has_side_effects=True, vmem_limit_bytes=40 * 1024 * 1024
         ),

time: 171 us -> 142 us (0.83)
  the two profiles are of different devices: /device:TPU:26 before, /device:TPU:0 now
where the time goes in v3:
time: 142 us
  Pallas kernels  130 us (92%)
  local copies, waits for them, and re-layouts  7.95 us (6%)
  other arithmetic  3.88 us (3%)
    pallas_call x1, Pallas kernels, sum_over_groups(): pl.pallas_call(functools.partial(sum_kernel, size, CUTS), out_shape=jax.S...  76.4 us
    pallas_call x1, Pallas kernels, section_terms(): pl.pallas_call(functools.partial(section_kernel, parts), out_shape=jax.Sh...  53.6 us
    unnamed x16, local copies, waits for them, and re-layouts  7.95 us
    convert_element_type x1, other arithmetic, shards(): sum_over_groups(terms.reshape(3 * head_cols, features)).astype(F32)  3.88 us

profile of v3, /device:TPU:0, one launch (start us, length us, event | category | flops | bytes accessed | tf_op | source)
XLA Modules:
  0.0 141.9 jit_solution(1295290372855950689)
XLA Ops:
  0.0 0.0 copy-start.1
  0.0 1.1 copy-done.1
  1.1 0.0 copy-start.2
  1.1 1.0 copy-done.2
  2.1 0.0 copy-start.3
  2.1 1.0 copy-done.3
  3.0 0.0 copy-start.4
  3.0 0.7 copy-done.4
  3.8 0.0 copy-start.5
  3.8 0.7 copy-done.5
  4.5 0.0 copy-start.6
  4.5 0.7 copy-done.6
  5.2 0.0 copy-start.7
  5.2 0.7 copy-done.7
  5.8 53.6 %shard_map.82 = bf16[3,512,1280]{2,1,0:T(8,128)(2,1)} custom-call(s32[2,4]{1,0:T(2,128)S(1)} %bitcast.8, s32[2,4]{1,0:T(2,128)S(1)} %bitcast.9, bf16[2,128,1280]{2,1,0:T(8,128)(2,1)S(1)} %copy-done.1, bf16[2,64,1280]{2,1,0:T(8,128)(2,1)S(1)} %copy-done.2, bf16[2,64,1280]{2,1,0:T(8,128)(2,1)S(1)} %copy-done.3, bf16[4,512,1280]{2,1,0:T(8,128)(2,1)} %bitcast.10, ...), custom_call_target="tpu_custom_call" | custom-call | tf_op jit(solution)/shard_map/pallas_call | solution.py:276
  59.5 0.0 copy-start
  59.5 2.1 %copy-done = bf16[3,512,1280]{2,1,0:T(8,128)(2,1)S(1)} copy-done((bf16[3,512,1280]{2,1,0:T(8,128)(2,1)S(1)}, bf16[3,512,1280]{2,1,0:T(8,128)(2,1)}, u32[]{:S(2)}) %copy-start) | copy-done | bytes 3932184
  61.6 76.4 %shard_map.83 = bf16[2,2,8,48,1280]{4,3,2,1,0:T(8,128)(2,1)S(1)} custom-call(bf16[2,2,8,48,1280]{4,3,2,1,0:T(8,128)(2,1)S(1)} %bitcast.7), custom_call_target="tpu_custom_call" | custom-call | tf_op jit(solution)/shard_map/pallas_call | solution.py:429
  138.0 3.9 %convert.1 = f32[1,3,512,1280]{3,2,1,0:T(8,128)} convert(bf16[1,3,512,1280]{3,2,1,0:T(8,128)(2,1)S(1)} %bitcast.6) | non-fusion elementwise | flops 1966080 | bytes 11796480 | tf_op jit(solution)/shard_map/convert_element_type | solution.py:451
Async XLA Ops:
  0.0 1.1 copy-start.1
  1.1 1.0 copy-start.2
  2.1 1.0 copy-start.3
  3.0 0.7 copy-start.4
  3.8 0.7 copy-start.5
  4.5 0.7 copy-start.6
  5.2 0.7 copy-start.7
  59.5 2.1 %copy-start = (bf16[3,512,1280]{2,1,0:T(8,128)(2,1)S(1)}, bf16[3,512,1280]{2,1,0:T(8,128)(2,1)}, u32[]{:S(2)}) copy-start(bf16[3,512,1280]{2,1,0:T(8,128)(2,1)} %shard_map.82) | copy-start | bytes 11796484

commit v4 on v3

--- a/solution.py
+++ b/solution.py
@@ -67,8 +67,8 @@
 
 
 def section_kernel(
-    parts, frame_lens, token_lens, frames, tokens, upstream, weights, gains, biases, terms,
-    full, normed, queries, key_rows, value_rows, context, probs, part, inbox, states, state_grad,
+    parts, frame_lens, token_lens, frames, tokens_in, upstream_in, weights_in, gains, biases,
+    terms, tokens, upstream, weights, local_sem, full, normed, queries, key_rows, value_rows, context, probs, part, inbox, states, state_grad,
     key_grad, value_grad, bias, dec_bias, dec_queries, dec_grad, dec_context,
     frame_send, frame_recv, pass_send, pass_recv, part_send, part_recv, state_send, state_recv,
 ):
@@ -80,6 +80,16 @@
     head_cols = weights.shape[1]
     heads = head_cols // HS
     scaling = 1.0 / math.sqrt(HS)
+
+    moves = [(frames.at[m], full.at[m, place]) for m in range(micro_count)]
+    moves += [(tokens_in, tokens), (upstream_in, upstream)]
+    moves += [(weights_in.at[i], weights.at[i]) for i in range(weights.shape[0])]
+    loads = [
+        pltpu.make_async_copy(source, target, local_sem.at[i])
+        for i, (source, target) in enumerate(moves)
+    ]
+    for load in loads:
+        load.start()
 
     barrier = pltpu.get_barrier_semaphore()
     for apart in range(parts):
@@ -230,8 +240,8 @@
         for m in range(micro_count):
             for apart in range(1, parts):
                 frame_copy(m, apart).start()
-        for m in range(micro_count):
-            full[m, place] = frames[m]
+        for load in loads:
+            load.wait()
         lax.fori_loop(0, micro_count, encoder_forward, 0)
         lax.fori_loop(0, micro_count, encoder_backward, 0)
         store_terms(context, state_grad)
@@ -244,8 +254,8 @@
 
     @pl.when(section == 1)
     def _():
-        for m in range(micro_count):
-            full[m, place] = frames[m]
+        for load in loads:
+            load.wait()
         rows, _ = standardize(flat(tokens[...]).astype(F32))
         token_rows = (rows * gains[1:2, :] + biases[1:2, :]).astype(BF16)
         small = (micro_count, token_count, head_cols)
@@ -277,9 +287,14 @@
         functools.partial(section_kernel, parts),
         out_shape=jax.ShapeDtypeStruct((3, head_cols, features), BF16),
         in_specs=[pl.BlockSpec(memory_space=pltpu.SMEM)] * 2
-        + [pl.BlockSpec(memory_space=pltpu.VMEM)] * 6,
+        + [pl.BlockSpec(memory_space=pl.ANY)] * 4
+        + [pl.BlockSpec(memory_space=pltpu.VMEM)] * 2,
         out_specs=pl.BlockSpec(memory_space=pltpu.VMEM),
         scratch_shapes=[
+            pltpu.VMEM(dec_states.shape, BF16),
+            pltpu.VMEM(out_grad.shape, BF16),
+            pltpu.VMEM(matrices.shape, BF16),
+            dma((micro_count + 2 + matrices.shape[0],)),
             pltpu.VMEM((micro_count, parts, shard_rows, features), BF16),
             wide,
             thin,
@@ -308,7 +323,7 @@
             dma((micro_count,)),
         ],
         compiler_params=pltpu.CompilerParams(
-            collective_id=1, has_side_effects=True, vmem_limit_bytes=52 * 1024 * 1024
+            collective_id=1, has_side_effects=True, vmem_limit_bytes=60 * 1024 * 1024
         ),
     )(
         frame_lengths[:, 0], token_lengths[:, 0], frames, dec_states, out_grad, matrices,
@@ -317,7 +332,7 @@
 
 
 def sum_kernel(
-    size, cuts, g_ref, out_ref, held, inbox, add_send, add_recv, back_send, back_recv
+    size, cuts, terms_ref, out_ref, g_ref, load_sem, held, inbox, add_send, add_recv, back_send, back_recv
 ):
     near = NEAR
     far = size // near
@@ -332,6 +347,8 @@
 
     ways = (1, -1)
     peers = [device_at(place + way) for way in ways]
+    load = pltpu.make_async_copy(terms_ref, g_ref, load_sem)
+    load.start()
 
     barrier = pltpu.get_barrier_semaphore()
     for peer in peers:
@@ -342,7 +359,7 @@
         return lax.rem(place + ways[d] * apart + 2 * size, size)
 
     def add_copy(d, c, step, first):
-        source = g_ref.at[d, c, block(d, 0)] if first else held.at[d, c, step - 1]
+        source = terms_ref.at[d, c, block(d, 0)] if first else held.at[d, c, step - 1]
         return pltpu.make_async_remote_copy(
             src_ref=source,
             dst_ref=inbox.at[d, c, step],
@@ -372,6 +389,7 @@
 
     for d, c in streams:
         add_copy(d, c, 0, True).start()
+    load.wait()
 
     def add_step(step, carry):
         for d, c in streams:
@@ -429,11 +447,13 @@
     out = pl.pallas_call(
         functools.partial(sum_kernel, size, CUTS),
         out_shape=jax.ShapeDtypeStruct(blocks.shape, BF16),
-        in_specs=[pl.BlockSpec(memory_space=pltpu.VMEM)],
+        in_specs=[pl.BlockSpec(memory_space=pl.ANY)],
         out_specs=pl.BlockSpec(memory_space=pltpu.VMEM),
-        scratch_shapes=[slots, slots, signals, signals, signals, signals],
+        scratch_shapes=[
+            pltpu.VMEM(blocks.shape, BF16), pltpu.SemaphoreType.DMA, slots, slots, signals, signals, signals, signals,
+        ],
         compiler_params=pltpu.CompilerParams(
-            collective_id=0, has_side_effects=True, vmem_limit_bytes=40 * 1024 * 1024
+            collective_id=0, has_side_effects=True, vmem_limit_bytes=60 * 1024 * 1024
         ),
     )(blocks)
     return out.reshape(padded, features)[:rows]

time: 142 us -> 137 us (0.965)
  local copies, waits for them, and re-layouts: 7.95 us -> 0 us
  other arithmetic: 3.88 us -> 6 us
    unnamed x16 -> x0, local copies, waits for them, and re-layouts: 7.95 us -> none
    pallas_call x1, Pallas kernels: 76.4 us -> 78.6 us  [sum_over_groups(): pl.pallas_call(functools.partial(sum_kernel, size, CUTS), out_shape=jax.S...]
    convert_element_type x1, other arithmetic: 3.88 us -> 6 us  [shards(): sum_over_groups(terms.reshape(3 * head_cols, features)).astype(F32)]
    pallas_call x1, Pallas kernels: 53.6 us -> 52.2 us  [section_terms(): pl.pallas_call(functools.partial(section_kernel, parts), out_shape=jax.Sh...]
where the time goes in v4:
time: 137 us
  Pallas kernels  131 us (96%)
  other arithmetic  6 us (4%)
    pallas_call x1, Pallas kernels, sum_over_groups(): pl.pallas_call(functools.partial(sum_kernel, size, CUTS), out_shape=jax.S...  78.6 us
    pallas_call x1, Pallas kernels, section_terms(): pl.pallas_call(functools.partial(section_kernel, parts), out_shape=jax.Sh...  52.2 us
    convert_element_type x1, other arithmetic, shards(): sum_over_groups(terms.reshape(3 * head_cols, features)).astype(F32)  6 us

profile of v4, /device:TPU:0, one launch (start us, length us, event | category | flops | bytes accessed | tf_op | source)
XLA Modules:
  0.0 136.8 jit_solution(14398827427261299331)
XLA Ops:
  0.0 52.2 %shard_map.82 = bf16[3,512,1280]{2,1,0:T(8,128)(2,1)} custom-call(s32[2,4]{1,0:T(2,128)} %bitcast.9, s32[2,4]{1,0:T(2,128)} %bitcast.10, bf16[2,128,1280]{2,1,0:T(8,128)(2,1)} %frames.1, bf16[2,64,1280]{2,1,0:T(8,128)(2,1)} %tokens_in.1, bf16[2,64,1280]{2,1,0:T(8,128)(2,1)} %upstream_in.1, bf16[4,512,1280]{2,1,0:T(8,128)(2,1)} %bitcast.8, f32[3,1280]{1,0:T(4,128)} %gains.1, ...), custom_call_target="tpu_custom_call" | custom-call | tf_op jit(solution)/shard_map/pallas_call | solution.py:286
  52.2 78.6 %shard_map.83 = bf16[2,2,8,48,1280]{4,3,2,1,0:T(8,128)(2,1)} custom-call(bf16[2,2,8,48,1280]{4,3,2,1,0:T(8,128)(2,1)} %bitcast.7), custom_call_target="tpu_custom_call" | custom-call | tf_op jit(solution)/shard_map/pallas_call | solution.py:447
  130.8 6.0 %convert.1 = f32[1,3,512,1280]{3,2,1,0:T(8,128)} convert(bf16[1,3,512,1280]{3,2,1,0:T(8,128)(2,1)} %bitcast.6) | non-fusion elementwise | flops 1966080 | bytes 11796480 | tf_op jit(solution)/shard_map/convert_element_type | solution.py:471

commit v5 on v4

--- a/solution.py
+++ b/solution.py
@@ -332,7 +332,7 @@
 
 
 def sum_kernel(
-    size, cuts, terms_ref, out_ref, g_ref, load_sem, held, inbox, add_send, add_recv, back_send, back_recv
+    size, cuts, g_ref, out_ref, held, inbox, add_send, add_recv, back_send, back_recv
 ):
     near = NEAR
     far = size // near
@@ -347,8 +347,6 @@
 
     ways = (1, -1)
     peers = [device_at(place + way) for way in ways]
-    load = pltpu.make_async_copy(terms_ref, g_ref, load_sem)
-    load.start()
 
     barrier = pltpu.get_barrier_semaphore()
     for peer in peers:
@@ -359,7 +357,7 @@
         return lax.rem(place + ways[d] * apart + 2 * size, size)
 
     def add_copy(d, c, step, first):
-        source = terms_ref.at[d, c, block(d, 0)] if first else held.at[d, c, step - 1]
+        source = g_ref.at[d, c, block(d, 0)] if first else held.at[d, c, step - 1]
         return pltpu.make_async_remote_copy(
             src_ref=source,
             dst_ref=inbox.at[d, c, step],
@@ -389,7 +387,6 @@
 
     for d, c in streams:
         add_copy(d, c, 0, True).start()
-    load.wait()
 
     def add_step(step, carry):
         for d, c in streams:
@@ -447,13 +444,11 @@
     out = pl.pallas_call(
         functools.partial(sum_kernel, size, CUTS),
         out_shape=jax.ShapeDtypeStruct(blocks.shape, BF16),
-        in_specs=[pl.BlockSpec(memory_space=pl.ANY)],
+        in_specs=[pl.BlockSpec(memory_space=pltpu.VMEM)],
         out_specs=pl.BlockSpec(memory_space=pltpu.VMEM),
-        scratch_shapes=[
-            pltpu.VMEM(blocks.shape, BF16), pltpu.SemaphoreType.DMA, slots, slots, signals, signals, signals, signals,
-        ],
+        scratch_shapes=[slots, slots, signals, signals, signals, signals],
         compiler_params=pltpu.CompilerParams(
-            collective_id=0, has_side_effects=True, vmem_limit_bytes=60 * 1024 * 1024
+            collective_id=0, has_side_effects=True, vmem_limit_bytes=40 * 1024 * 1024
         ),
     )(blocks)
     return out.reshape(padded, features)[:rows]

time: 137 us -> 135 us (0.985)
  other arithmetic: 6 us -> 3.88 us
  local copies, waits for them, and re-layouts: 0 us -> 2.11 us
  Pallas kernels: 131 us -> 129 us
    pallas_call x1, Pallas kernels: 78.6 us -> 76.4 us  [sum_over_groups(): pl.pallas_call(functools.partial(sum_kernel, size, CUTS), out_shape=jax.S...]
    convert_element_type x1, other arithmetic: 6 us -> 3.88 us  [shards(): sum_over_groups(terms.reshape(3 * head_cols, features)).astype(F32)]
    unnamed x0 -> x2, local copies, waits for them, and re-layouts: none -> 2.11 us
where the time goes in v5:
time: 135 us
  Pallas kernels  129 us (96%)
  other arithmetic  3.88 us (3%)
  local copies, waits for them, and re-layouts  2.11 us (2%)
    pallas_call x1, Pallas kernels, sum_over_groups(): pl.pallas_call(functools.partial(sum_kernel, size, CUTS), out_shape=jax.S...  76.4 us
    pallas_call x1, Pallas kernels, section_terms(): pl.pallas_call(functools.partial(section_kernel, parts), out_shape=jax.Sh...  52.2 us
    convert_element_type x1, other arithmetic, shards(): sum_over_groups(terms.reshape(3 * head_cols, features)).astype(F32)  3.88 us

profile of v5, /device:TPU:0, one launch (start us, length us, event | category | flops | bytes accessed | tf_op | source)
XLA Modules:
  0.0 134.6 jit_solution(9194101524040083184)
XLA Ops:
  0.0 52.2 %shard_map.82 = bf16[3,512,1280]{2,1,0:T(8,128)(2,1)} custom-call(s32[2,4]{1,0:T(2,128)} %bitcast.9, s32[2,4]{1,0:T(2,128)} %bitcast.10, bf16[2,128,1280]{2,1,0:T(8,128)(2,1)} %frames.1, bf16[2,64,1280]{2,1,0:T(8,128)(2,1)} %tokens_in.1, bf16[2,64,1280]{2,1,0:T(8,128)(2,1)} %upstream_in.1, bf16[4,512,1280]{2,1,0:T(8,128)(2,1)} %bitcast.8, f32[3,1280]{1,0:T(4,128)} %gains.1, ...), custom_call_target="tpu_custom_call" | custom-call | tf_op jit(solution)/shard_map/pallas_call | solution.py:286
  52.2 0.0 copy-start
  52.2 2.1 %copy-done = bf16[3,512,1280]{2,1,0:T(8,128)(2,1)S(1)} copy-done((bf16[3,512,1280]{2,1,0:T(8,128)(2,1)S(1)}, bf16[3,512,1280]{2,1,0:T(8,128)(2,1)}, u32[]{:S(2)}) %copy-start) | copy-done | bytes 3932184
  54.3 76.4 %shard_map.83 = bf16[2,2,8,48,1280]{4,3,2,1,0:T(8,128)(2,1)S(1)} custom-call(bf16[2,2,8,48,1280]{4,3,2,1,0:T(8,128)(2,1)S(1)} %bitcast.7), custom_call_target="tpu_custom_call" | custom-call | tf_op jit(solution)/shard_map/pallas_call | solution.py:444
  130.7 3.9 %convert.1 = f32[1,3,512,1280]{3,2,1,0:T(8,128)} convert(bf16[1,3,512,1280]{3,2,1,0:T(8,128)(2,1)S(1)} %bitcast.6) | non-fusion elementwise | flops 1966080 | bytes 11796480 | tf_op jit(solution)/shard_map/convert_element_type | solution.py:466
Async XLA Ops:
  52.2 2.1 %copy-start = (bf16[3,512,1280]{2,1,0:T(8,128)(2,1)S(1)}, bf16[3,512,1280]{2,1,0:T(8,128)(2,1)}, u32[]{:S(2)}) copy-start(bf16[3,512,1280]{2,1,0:T(8,128)(2,1)} %shard_map.82) | copy-start | bytes 11796484
